TPU v7x, 32 devices: a whole 2x2x4 slice. The times are simulated.
32 devices in a mesh: blk: 8 (over y, x, core), row: 4 (over z).
Axes of the slice: x: 2, y: 2, z: 4, core: 2. Of those that a mesh axis runs over, the one named last changes fastest.
Arguments:
- gauss_params: float32 [14, 16384], P(None, ('blk', 'row')), may hold values from -7 to 10, as said below
- tile_ids: int32 [512], P(('blk', 'row')), may hold values from 0 to 511, as said below
- tile_lists: int32 [512, 1024], P(('blk', 'row')), may hold values from -1 to 16383, as said below
Outputs:
- pixel_colors: float32 [512, 3, 256], P(('blk', 'row'))
- transmittance: float32 [512, 256], P(('blk', 'row'))
- significance: float32 [16384], P(('blk', 'row'))
Inputs may be any that keep to these rules, and one draw needn't show every extreme that they name: `gauss_params`: rows 0 to 2 are a mean in camera coordinates whose z lies between 2 and 10; rows 3 to 5 are logarithms of scales; rows 6 to 9 a quaternion (w, x, y, z) with w between 0.5 and 1.5 and the others between -1 and 1; row 10 an opacity logit; rows 11 to 13 color coefficients. `tile_ids`: each of the 512 window tiles is held by exactly one slot. `tile_lists`: A list holds distinct Gaussian indices in ascending order of the mean's z, followed by -1 entries. The lists of the 16 slots of one device name at most 200 distinct indices of any one block s * 512 to (s + 1) * 512 - 1, and some device names exactly 200 of some block.
All inputs are finite; a program needn't handle non-finite values.
Results may differ from a plain program's by a relative error of at most 0.0003.
Values sent between devices are 32-bit elements; how exact they have to be, the bound alone decides.
No kernel may reach another device: no remote copies, remote signals or barrier semaphores. Data moves between devices by JAX's collectives and lax.ppermute only.
A program may use at most 128 MiB of HBM per device.

v0:
```python
import jax
import jax.numpy as jnp
from jax import lax
from jax.sharding import PartitionSpec as P

TILE_SIDE = 16
SCREEN_W = 3840
SCREEN_H = 2160
WIN_X = 64
BLOCK = 256


FOCAL = 3200.0
DILATION = 0.3
SH_ZERO = 0.28209479177387814
ALPHA_CAP = 0.99


def project(params):
    mean_x = params[0]
    mean_y = params[1]
    mean_z = params[2]
    scales = jnp.exp(params[3:6])
    quaternion = params[6:10]
    quaternion = quaternion / jnp.sqrt(jnp.sum(quaternion * quaternion, axis=0))
    quat_w = quaternion[0]
    quat_x = quaternion[1]
    quat_y = quaternion[2]
    quat_z = quaternion[3]
    rotation = [
        [
            1.0 - 2.0 * (quat_y * quat_y + quat_z * quat_z),
            2.0 * (quat_x * quat_y - quat_w * quat_z),
            2.0 * (quat_x * quat_z + quat_w * quat_y),
        ],
        [
            2.0 * (quat_x * quat_y + quat_w * quat_z),
            1.0 - 2.0 * (quat_x * quat_x + quat_z * quat_z),
            2.0 * (quat_y * quat_z - quat_w * quat_x),
        ],
        [
            2.0 * (quat_x * quat_z - quat_w * quat_y),
            2.0 * (quat_y * quat_z + quat_w * quat_x),
            1.0 - 2.0 * (quat_x * quat_x + quat_y * quat_y),
        ],
    ]
    inv_z = 1.0 / mean_z
    jac_a = FOCAL * inv_z
    jac_x = -FOCAL * mean_x * inv_z * inv_z
    jac_y = -FOCAL * mean_y * inv_z * inv_z
    first_row = [
        (jac_a * rotation[0][column_k] + jac_x * rotation[2][column_k]) * scales[column_k]
        for column_k in range(3)
    ]
    second_row = [
        (jac_a * rotation[1][column_k] + jac_y * rotation[2][column_k]) * scales[column_k]
        for column_k in range(3)
    ]
    cov_a = (
        first_row[0] * first_row[0]
        + first_row[1] * first_row[1]
        + first_row[2] * first_row[2]
        + DILATION
    )
    cov_b = (
        first_row[0] * second_row[0] + first_row[1] * second_row[1] + first_row[2] * second_row[2]
    )
    cov_c = (
        second_row[0] * second_row[0]
        + second_row[1] * second_row[1]
        + second_row[2] * second_row[2]
        + DILATION
    )
    determinant = cov_a * cov_c - cov_b * cov_b
    center_u = FOCAL * mean_x * inv_z + SCREEN_W / 2
    center_v = FOCAL * mean_y * inv_z + SCREEN_H / 2
    opacity = jax.nn.sigmoid(params[10])
    radiance = jnp.maximum(SH_ZERO * params[11:14] + 0.5, 0.0)
    shape_rows = jnp.stack(
        [
            center_u,
            center_v,
            cov_c / determinant,
            -cov_b / determinant,
            cov_a / determinant,
            opacity,
        ]
    )
    return jnp.concatenate([shape_rows, radiance], axis=0)


def place_records(entry_table, piece_rec, flat_ids):
    width = piece_rec.shape[1]
    inside = (flat_ids >= 0) & (flat_ids < width)
    fetched = jnp.take(piece_rec, jnp.clip(flat_ids, 0, width - 1), axis=1)
    return jnp.where(inside[None, :], fetched, entry_table)


def pixel_grid(tile_ids, off_x, off_y):
    column = (tile_ids % WIN_X).astype(jnp.float32)
    tile_row = (tile_ids // WIN_X).astype(jnp.float32)
    within = jnp.arange(TILE_SIDE * TILE_SIDE, dtype=jnp.int32)
    inner_x = (within % TILE_SIDE).astype(jnp.float32)
    inner_y = (within // TILE_SIDE).astype(jnp.float32)
    pixel_x = off_x + column[:, None] * TILE_SIDE + inner_x[None, :] + 0.5
    pixel_y = off_y + tile_row[:, None] * TILE_SIDE + inner_y[None, :] + 0.5
    return (pixel_x, pixel_y)


def blend_block(carry_state, block_rec, pixel_x, pixel_y):
    transmit, radiance = carry_state
    delta_x = pixel_x[:, :, None] - block_rec[0][:, None, :]
    delta_y = pixel_y[:, :, None] - block_rec[1][:, None, :]
    exponent = (
        -0.5
        * (
            block_rec[2][:, None, :] * delta_x * delta_x
            + block_rec[4][:, None, :] * delta_y * delta_y
        )
        - block_rec[3][:, None, :] * delta_x * delta_y
    )
    alphas = jnp.minimum(ALPHA_CAP, block_rec[5][:, None, :] * jnp.exp(exponent))
    log_keep = jnp.log1p(-alphas)
    before = jnp.cumsum(log_keep, axis=2) - log_keep
    weight = transmit[:, :, None] * jnp.exp(before) * alphas
    radiance = radiance + jnp.einsum(
        "npg,cng->ncp", weight, block_rec[6:9], precision=lax.Precision.HIGHEST
    )
    transmit = transmit * jnp.exp(jnp.sum(log_keep, axis=2))
    return ((transmit, radiance), jnp.sum(weight, axis=1) / weight.shape[1])


def render_group(operands):
    tables, pixel_x, pixel_y = operands
    count_here = tables.shape[1]
    pixels = pixel_x.shape[1]
    carry_state = (
        jnp.ones((count_here, pixels), jnp.float32),
        jnp.zeros((count_here, 3, pixels), jnp.float32),
    )
    block_sums = []
    for block_index in range(tables.shape[2] // BLOCK):
        block_rec = tables[:, :, block_index * BLOCK : (block_index + 1) * BLOCK]
        busy = jnp.any(block_rec[5] > 0.0)
        carry_state, block_sum = lax.cond(
            busy,
            lambda state_in: blend_block(state_in, block_rec, pixel_x, pixel_y),
            lambda state_in: (state_in, jnp.zeros((count_here, BLOCK), jnp.float32)),
            carry_state,
        )
        block_sums.append(block_sum)
    return (carry_state[1], carry_state[0], jnp.concatenate(block_sums, axis=1))


def render(entry_table, tile_ids, off_x, off_y):
    pixel_x, pixel_y = pixel_grid(tile_ids, off_x, off_y)
    tile_count = entry_table.shape[1]
    list_len = entry_table.shape[2]
    grouping = 4
    groups = tile_count // grouping
    grouped = entry_table.reshape(9, groups, grouping, list_len).transpose(1, 0, 2, 3)
    shaped_x = pixel_x.reshape(groups, grouping, -1)
    shaped_y = pixel_y.reshape(groups, grouping, -1)
    radiance, transmit, weight_sums = lax.map(render_group, (grouped, shaped_x, shaped_y))
    return (
        radiance.reshape(tile_count, 3, -1),
        transmit.reshape(tile_count, -1),
        weight_sums.reshape(tile_count, list_len),
    )


def local(gauss_params, tile_ids, tile_lists):
    tiles_here = tile_lists.shape[0]
    list_len = tile_lists.shape[1]
    flat_ids = tile_lists.reshape(-1)
    devices = lax.axis_size(("blk", "row"))
    shard_rows = gauss_params.shape[1]
    blank_table = jnp.zeros((9, flat_ids.shape[0]), jnp.float32)
    entry_table = place_records(
        blank_table,
        project(lax.all_gather(gauss_params, ("blk", "row"), axis=1, tiled=True)),
        flat_ids,
    )
    tiles_total = tiles_here * devices
    win_y = tiles_total // WIN_X
    off_x = (SCREEN_W - WIN_X * TILE_SIDE) // 2
    off_y = (SCREEN_H - win_y * TILE_SIDE) // 2
    pixel_colors, transmittance, weight_sums = render(
        entry_table.reshape(9, tiles_here, list_len), tile_ids, off_x, off_y
    )
    flat_weights = weight_sums.reshape(-1)
    row_count = lax.axis_size(("blk", "row")) * shard_rows
    inside = (flat_ids >= 0) & (flat_ids < row_count)
    seg_ids = jnp.where(inside, flat_ids, row_count)
    significance = lax.psum_scatter(
        jax.ops.segment_sum(flat_weights, seg_ids, num_segments=row_count + 1)[:row_count],
        ("blk", "row"),
        scatter_dimension=0,
        tiled=True,
    )
    return (pixel_colors, transmittance, significance)


def solution(mesh):
    return jax.shard_map(
        local,
        mesh=mesh,
        in_specs=(P(None, ("blk", "row")), P(("blk", "row")), P(("blk", "row"), None)),
        out_specs=(P(("blk", "row"), None, None), P(("blk", "row"), None), P(("blk", "row"))),
        check_vma=False,
    )
```

profile of v0, /device:TPU:0, one launch (start us, length us, event | category | flops | bytes accessed | tf_op | source)
XLA Modules:
  0.0 564.5 jit_solution(14803703770927057816)
XLA Ops:
  7.2 78.8 %all_gather.3 = f32[14,16384]{1,0:T(8,128)S(1)} all-gather(f32[14,512]{1,0:T(8,128)} %param.13), channel_id=1, replica_groups=mesh['blk'=8,'row'=4] {'blk','row'}, dimensions={1}, use_global_device_ids=true | all-gather | bytes 946176 | tf_op jit(solution)/shard_map/all_gather | solution.py:181
  86.9 0.9 add_multiply_fusion.4
  87.8 0.9 add_multiply_fusion.6
  88.7 0.9 broadcast_clamp_fusion.1
  89.6 0.9 compare_and_fusion.1
  91.0 1.4 concatenate.6
  92.4 4.7 copy.178
  97.4 57.8 %gather_fusion = f32[16384,9]{1,0:T(8,128)} fusion(f32[9,16384]{0,1:T(8,128)} %copy.178, s32[16384]{0:T(1024)S(1)} %broadcast_clamp_fusion), kind=kCustom, calls=%fused_computation | custom fusion | bytes 1245184 | tf_op jit(solution)/shard_map/jit(_take)/gather | solution.py:95
  155.2 5.2 copy.179
  160.7 1.2 select_bitcast_fusion
  162.0 143.4 %while.14 = (s32[]{:T(128)}, f32[4,4,3,256]{3,2,1,0:T(4,128)S(1)}, f32[4,4,256]{2,1,0:T(4,128)S(1)}, f32[4,4,1024]{2,1,0:T(4,128)S(1)}, f32[4,9,4,1024]{3,1,2,0:...) while((s32[]{:T(128)}, f32[4,4,3,256]{3,2,1,0:T(4,128)S(1)}, ...), condition=%wide.region_30.31_spmd, body=%wide.region_1.30_spmd.sunk | while | flops 223911936 | bytes 35516848 | solution.py:164
  162.2 1.0 dynamic-slice_bitcast_fusion.5
  163.2 0.8 compare_reduce_fusion.5
  164.6 13.3 %conditional.8 = (f32[4,256]{1,0:T(4,128)S(1)}, f32[4,3,256]{2,1,0:T(4,128)S(1)}, f32[4,256]{1,0:T(4,128)S(1)}) conditional(s32[]{:T(128)} %convert_element_type.51, () %tuple.125, (f32[9,4,1024]{2,0,1:T(8,128)S(1)}, f32[4,256]{1,0:T(4,128)S(1)}, f32[4,256]{1,0:T(4,128)S(1)}) %tuple.126), branch_computations={%region_6.6_spmd, %region_7.11_spmd} | conditional | flops 55576576 | bytes 8757276 | solution.py:145
  165.6 3.9 fusion.14
  169.6 6.0 %multiply_reduce_fusion = (f32[4,2,128]{1,2,0:T(8,128)S(1)}, f32[4,256,2,128]{1,2,3,0:T(2,128)S(1)}) fusion(f32[4,256,2,128]{1,2,3,0:T(2,128)S(1)} %fusion.14, f32[4,256,2]{1,2,0:T(2,128)S(1)} %slice.226, f32[4,2,128]{1,2,0:T(8,128)S(1)} %copy.147, f32[4,2,128]{1,2,0:T(8,128)S(1)} %copy.146, f32[4,256]{1,0:T(4,128)S(1)} %get-tuple-element.82, ...), kind=kLoop, calls=%fused_computation.30 | loop fusion | flops 4717568 | bytes 2142208 | tf_op jit(solution)/shard_map/while/body/eval_jaxpr/cond/branch_1_fun/reduce_sum | solution.py:130
  175.7 1.4 fusion.13
  177.1 0.7 convolution_bitcast_fusion
  178.5 14.4 %conditional.9 = (f32[4,256]{1,0:T(4,128)S(1)}, f32[4,3,256]{2,1,0:T(4,128)S(1)}, f32[4,256]{1,0:T(4,128)S(1)}) conditional(s32[]{:T(128)} %convert_element_type.50, (f32[4,256]{1,0:T(4,128)S(1)}, f32[4,3,256]{2,1,0:T(4,128)S(1)}) %tuple.127, (f32[9,4,1024]{2,0,1:T(8,128)S(1)}, f32[4,256]{1,0:T(4,128)S(1)}, f32[4,256]{1,0:T(4,128)S(1)}, ...), branch_computations={%region_12.12_spmd, %region_13.17_spmd} | conditional | flops 56104960 | bytes 8785948 | solution.py:145
  179.5 3.9 fusion.33
  183.5 7.0 %multiply_reduce_fusion.1 = (f32[4,2,128]{1,2,0:T(8,128)S(1)}, f32[4,256,2,128]{1,2,3,0:T(2,128)S(1)}) fusion(f32[4,256]{1,0:T(4,128)S(1)} %get-tuple-element.85, f32[4,256,2,128]{1,2,3,0:T(2,128)S(1)} %fusion.33, f32[4,256,2]{1,2,0:T(2,128)S(1)} %slice.228, f32[4,2,128]{1,2,0:T(8,128)S(1)} %copy.156, f32[4,2,128]{1,2,0:T(8,128)S(1)} %copy.155, ...), kind=kLoop, calls=%fused_computation.75 | loop fusion | flops 4979712 | bytes 2146304 | tf_op jit(solution)/shard_map/while/body/eval_jaxpr/cond/branch_1_fun/reduce_sum | solution.py:130
  190.7 1.5 fusion.32
  192.1 0.7 fusion.17
  194.4 1.0 dynamic-slice_bitcast_fusion.5
  195.4 0.8 compare_reduce_fusion.5
  196.8 13.3 %conditional.8 = (f32[4,256]{1,0:T(4,128)S(1)}, f32[4,3,256]{2,1,0:T(4,128)S(1)}, f32[4,256]{1,0:T(4,128)S(1)}) conditional(s32[]{:T(128)} %convert_element_type.51, () %tuple.125, (f32[9,4,1024]{2,0,1:T(8,128)S(1)}, f32[4,256]{1,0:T(4,128)S(1)}, f32[4,256]{1,0:T(4,128)S(1)}) %tuple.126), branch_computations={%region_6.6_spmd, %region_7.11_spmd} | conditional | flops 55576576 | bytes 8757276 | solution.py:145
  197.8 3.9 fusion.14
  201.7 6.0 %multiply_reduce_fusion = (f32[4,2,128]{1,2,0:T(8,128)S(1)}, f32[4,256,2,128]{1,2,3,0:T(2,128)S(1)}) fusion(f32[4,256,2,128]{1,2,3,0:T(2,128)S(1)} %fusion.14, f32[4,256,2]{1,2,0:T(2,128)S(1)} %slice.226, f32[4,2,128]{1,2,0:T(8,128)S(1)} %copy.147, f32[4,2,128]{1,2,0:T(8,128)S(1)} %copy.146, f32[4,256]{1,0:T(4,128)S(1)} %get-tuple-element.82, ...), kind=kLoop, calls=%fused_computation.30 | loop fusion | flops 4717568 | bytes 2142208 | tf_op jit(solution)/shard_map/while/body/eval_jaxpr/cond/branch_1_fun/reduce_sum | solution.py:130
  207.9 1.4 fusion.13
  210.7 14.4 %conditional.9 = (f32[4,256]{1,0:T(4,128)S(1)}, f32[4,3,256]{2,1,0:T(4,128)S(1)}, f32[4,256]{1,0:T(4,128)S(1)}) conditional(s32[]{:T(128)} %convert_element_type.50, (f32[4,256]{1,0:T(4,128)S(1)}, f32[4,3,256]{2,1,0:T(4,128)S(1)}) %tuple.127, (f32[9,4,1024]{2,0,1:T(8,128)S(1)}, f32[4,256]{1,0:T(4,128)S(1)}, f32[4,256]{1,0:T(4,128)S(1)}, ...), branch_computations={%region_12.12_spmd, %region_13.17_spmd} | conditional | flops 56104960 | bytes 8785948 | solution.py:145
  211.7 3.9 fusion.33
  215.7 7.0 %multiply_reduce_fusion.1 = (f32[4,2,128]{1,2,0:T(8,128)S(1)}, f32[4,256,2,128]{1,2,3,0:T(2,128)S(1)}) fusion(f32[4,256]{1,0:T(4,128)S(1)} %get-tuple-element.85, f32[4,256,2,128]{1,2,3,0:T(2,128)S(1)} %fusion.33, f32[4,256,2]{1,2,0:T(2,128)S(1)} %slice.228, f32[4,2,128]{1,2,0:T(8,128)S(1)} %copy.156, f32[4,2,128]{1,2,0:T(8,128)S(1)} %copy.155, ...), kind=kLoop, calls=%fused_computation.75 | loop fusion | flops 4979712 | bytes 2146304 | tf_op jit(solution)/shard_map/while/body/eval_jaxpr/cond/branch_1_fun/reduce_sum | solution.py:130
  222.9 1.5 fusion.32
  224.3 0.7 fusion.17
  225.9 14.4 %conditional.10 = (f32[4,256]{1,0:T(4,128)S(1)}, f32[4,3,256]{2,1,0:T(4,128)S(1)}, f32[4,256]{1,0:T(4,128)S(1)}) conditional(s32[]{:T(128)} %convert_element_type.49, (f32[4,256]{1,0:T(4,128)S(1)}, f32[4,3,256]{2,1,0:T(4,128)S(1)}) %tuple.129, (f32[9,4,1024]{2,0,1:T(8,128)S(1)}, f32[4,256]{1,0:T(4,128)S(1)}, f32[4,256]{1,0:T(4,128)S(1)}, ...), branch_computations={%region_18.18_spmd, %region_19.23_spmd} | conditional | flops 56104960 | bytes 8785948 | solution.py:145
  226.9 3.9 fusion.52
  230.8 7.0 %multiply_reduce_fusion.2 = (f32[4,2,128]{1,2,0:T(8,128)S(1)}, f32[4,256,2,128]{1,2,3,0:T(2,128)S(1)}) fusion(f32[4,256]{1,0:T(4,128)S(1)} %get-tuple-element.92, f32[4,256,2,128]{1,2,3,0:T(2,128)S(1)} %fusion.52, f32[4,256,2]{1,2,0:T(2,128)S(1)} %slice.230, f32[4,2,128]{1,2,0:T(8,128)S(1)} %copy.165, f32[4,2,128]{1,2,0:T(8,128)S(1)} %copy.164, ...), kind=kLoop, calls=%fused_computation.121 | loop fusion | flops 4979712 | bytes 2146304 | tf_op jit(solution)/shard_map/while/body/eval_jaxpr/cond/branch_1_fun/reduce_sum | solution.py:130
  238.0 1.5 fusion.51
  239.5 0.7 fusion.36
  241.0 1.0 dynamic-slice_bitcast_fusion.5
  242.0 0.8 compare_reduce_fusion.5
  243.4 13.3 %conditional.8 = (f32[4,256]{1,0:T(4,128)S(1)}, f32[4,3,256]{2,1,0:T(4,128)S(1)}, f32[4,256]{1,0:T(4,128)S(1)}) conditional(s32[]{:T(128)} %convert_element_type.51, () %tuple.125, (f32[9,4,1024]{2,0,1:T(8,128)S(1)}, f32[4,256]{1,0:T(4,128)S(1)}, f32[4,256]{1,0:T(4,128)S(1)}) %tuple.126), branch_computations={%region_6.6_spmd, %region_7.11_spmd} | conditional | flops 55576576 | bytes 8757276 | solution.py:145
  244.4 3.9 fusion.14
  248.4 6.0 %multiply_reduce_fusion = (f32[4,2,128]{1,2,0:T(8,128)S(1)}, f32[4,256,2,128]{1,2,3,0:T(2,128)S(1)}) fusion(f32[4,256,2,128]{1,2,3,0:T(2,128)S(1)} %fusion.14, f32[4,256,2]{1,2,0:T(2,128)S(1)} %slice.226, f32[4,2,128]{1,2,0:T(8,128)S(1)} %copy.147, f32[4,2,128]{1,2,0:T(8,128)S(1)} %copy.146, f32[4,256]{1,0:T(4,128)S(1)} %get-tuple-element.82, ...), kind=kLoop, calls=%fused_computation.30 | loop fusion | flops 4717568 | bytes 2142208 | tf_op jit(solution)/shard_map/while/body/eval_jaxpr/cond/branch_1_fun/reduce_sum | solution.py:130
  254.5 1.4 fusion.13
  257.3 14.4 %conditional.9 = (f32[4,256]{1,0:T(4,128)S(1)}, f32[4,3,256]{2,1,0:T(4,128)S(1)}, f32[4,256]{1,0:T(4,128)S(1)}) conditional(s32[]{:T(128)} %convert_element_type.50, (f32[4,256]{1,0:T(4,128)S(1)}, f32[4,3,256]{2,1,0:T(4,128)S(1)}) %tuple.127, (f32[9,4,1024]{2,0,1:T(8,128)S(1)}, f32[4,256]{1,0:T(4,128)S(1)}, f32[4,256]{1,0:T(4,128)S(1)}, ...), branch_computations={%region_12.12_spmd, %region_13.17_spmd} | conditional | flops 56104960 | bytes 8785948 | solution.py:145
  258.3 3.9 fusion.33
  262.3 7.0 %multiply_reduce_fusion.1 = (f32[4,2,128]{1,2,0:T(8,128)S(1)}, f32[4,256,2,128]{1,2,3,0:T(2,128)S(1)}) fusion(f32[4,256]{1,0:T(4,128)S(1)} %get-tuple-element.85, f32[4,256,2,128]{1,2,3,0:T(2,128)S(1)} %fusion.33, f32[4,256,2]{1,2,0:T(2,128)S(1)} %slice.228, f32[4,2,128]{1,2,0:T(8,128)S(1)} %copy.156, f32[4,2,128]{1,2,0:T(8,128)S(1)} %copy.155, ...), kind=kLoop, calls=%fused_computation.75 | loop fusion | flops 4979712 | bytes 2146304 | tf_op jit(solution)/shard_map/while/body/eval_jaxpr/cond/branch_1_fun/reduce_sum | solution.py:130
  269.5 1.5 fusion.32
  270.9 0.7 fusion.17
  273.2 1.0 dynamic-slice_bitcast_fusion.5
  274.2 0.8 compare_reduce_fusion.5
  275.6 13.3 %conditional.8 = (f32[4,256]{1,0:T(4,128)S(1)}, f32[4,3,256]{2,1,0:T(4,128)S(1)}, f32[4,256]{1,0:T(4,128)S(1)}) conditional(s32[]{:T(128)} %convert_element_type.51, () %tuple.125, (f32[9,4,1024]{2,0,1:T(8,128)S(1)}, f32[4,256]{1,0:T(4,128)S(1)}, f32[4,256]{1,0:T(4,128)S(1)}) %tuple.126), branch_computations={%region_6.6_spmd, %region_7.11_spmd} | conditional | flops 55576576 | bytes 8757276 | solution.py:145
  276.6 3.9 fusion.14
  280.5 6.0 %multiply_reduce_fusion = (f32[4,2,128]{1,2,0:T(8,128)S(1)}, f32[4,256,2,128]{1,2,3,0:T(2,128)S(1)}) fusion(f32[4,256,2,128]{1,2,3,0:T(2,128)S(1)} %fusion.14, f32[4,256,2]{1,2,0:T(2,128)S(1)} %slice.226, f32[4,2,128]{1,2,0:T(8,128)S(1)} %copy.147, f32[4,2,128]{1,2,0:T(8,128)S(1)} %copy.146, f32[4,256]{1,0:T(4,128)S(1)} %get-tuple-element.82, ...), kind=kLoop, calls=%fused_computation.30 | loop fusion | flops 4717568 | bytes 2142208 | tf_op jit(solution)/shard_map/while/body/eval_jaxpr/cond/branch_1_fun/reduce_sum | solution.py:130
  286.7 1.4 fusion.13
  289.5 14.4 %conditional.9 = (f32[4,256]{1,0:T(4,128)S(1)}, f32[4,3,256]{2,1,0:T(4,128)S(1)}, f32[4,256]{1,0:T(4,128)S(1)}) conditional(s32[]{:T(128)} %convert_element_type.50, (f32[4,256]{1,0:T(4,128)S(1)}, f32[4,3,256]{2,1,0:T(4,128)S(1)}) %tuple.127, (f32[9,4,1024]{2,0,1:T(8,128)S(1)}, f32[4,256]{1,0:T(4,128)S(1)}, f32[4,256]{1,0:T(4,128)S(1)}, ...), branch_computations={%region_12.12_spmd, %region_13.17_spmd} | conditional | flops 56104960 | bytes 8785948 | solution.py:145
  290.5 3.9 fusion.33
  294.5 7.0 %multiply_reduce_fusion.1 = (f32[4,2,128]{1,2,0:T(8,128)S(1)}, f32[4,256,2,128]{1,2,3,0:T(2,128)S(1)}) fusion(f32[4,256]{1,0:T(4,128)S(1)} %get-tuple-element.85, f32[4,256,2,128]{1,2,3,0:T(2,128)S(1)} %fusion.33, f32[4,256,2]{1,2,0:T(2,128)S(1)} %slice.228, f32[4,2,128]{1,2,0:T(8,128)S(1)} %copy.156, f32[4,2,128]{1,2,0:T(8,128)S(1)} %copy.155, ...), kind=kLoop, calls=%fused_computation.75 | loop fusion | flops 4979712 | bytes 2146304 | tf_op jit(solution)/shard_map/while/body/eval_jaxpr/cond/branch_1_fun/reduce_sum | solution.py:130
  301.7 1.5 fusion.32
  303.1 0.7 fusion.17
  305.4 102.3 %scatter_custom_fusion = f32[16385]{0:T(1024)S(1)} fusion(s32[16384]{0:T(1024)S(1)} %bitcast.202, f32[16384]{0:T(1024)S(1)} %bitcast.205, f32[]{:T(128)} %constant.158.clone.1), kind=kCustom, calls=%fused_computation.229 | custom fusion | flops 16384 | bytes 65544 | tf_op jit(solution)/shard_map/scatter-add | solution.py:196
  409.6 146.8 %all-reduce.3.cloned.1.call-done = f32[16384]{0:T(1024)} async-done(((f32[16384]{0:T(1024)}), f32[16384]{0:T(1024)}) %all-reduce.3.cloned.1.call-update) | async-done | bytes 65552
  556.3 1.3 dynamic-slice
  (218 shorter events, 17.3 us)
Async XLA Ops:
  7.2 549.1 %all-reduce.3.cloned.1.call-start = ((), (), s32[]{:S(2)}) async-start(), calls=%async_computation | async-start | bytes 131072
  86.0 11.1 %copy-start = (s32[16,1024]{1,0:T(8,128)S(1)}, s32[16,1024]{1,0:T(8,128)}, u32[]{:S(2)}) copy-start(s32[16,1024]{1,0:T(8,128)} %param.15) | copy-start | bytes 196612
  97.4 63.1 %copy-start.1 = (s32[16]{0:T(128)S(1)}, s32[16]{0:T(128)}, u32[]{:S(2)}) copy-start(s32[16]{0:T(128)} %param.14) | copy-start | bytes 196
Sparse Core Ops, SparseCore 0:
  408.4 147.8 all-reduce.2
where the time goes:
time: 569 us; the launch traced here: 564 us
  other arithmetic  220 us (39%)
  waiting for transfers between devices  147 us (26%)
  local copies, waits for them, and re-layouts  86.9 us (15%)
  blocking collectives  78.8 us (14%)
  between operations  14.2 us (2%)
  loops' own time  12.3 us (2%)
  matrix products  6 us (1%)
    unnamed x2, waiting for transfers between devices  147 us
    scatter-add x1, other arithmetic, local(): jax.ops.segment_sum(flat_weights, seg_ids, num_segments=row_count + 1)  102 us
    all_gather x1, blocking collectives, local(): lax.all_gather(gauss_params, ('blk', 'row'), axis=1, tiled=True)  78.8 us
    gather x2, local copies, waits for them, and re-layouts, place_records(): fetched = jnp.take(piece_rec, jnp.clip(flat_ids, 0, width - 1), axis=1)  63 us
    reduce_sum x9, other arithmetic, blend_block(): return ((transmit, radiance), jnp.sum(weight, axis=1) / weight.shape[1])  59.1 us
    another operation x18, other arithmetic  35.5 us
    mul x9, other arithmetic, blend_block(): weight = transmit[:, :, None] * jnp.exp(before) * alphas  12.8 us
  transfers between devices with their start and end apart: 1, of which 1 were waited for; matrix products, arithmetic and copies ran while one was open for 0% of the time, Pallas kernels for 0%

commit v1 on v0

v1 whole, which is shorter than its diff:
```python
import functools

import jax
import jax.numpy as jnp
from jax import lax
from jax.experimental import pallas as pl
from jax.experimental.pallas import tpu as pltpu
from jax.sharding import PartitionSpec as P

TILE_SIDE = 16
SCREEN_W = 3840
SCREEN_H = 2160
WIN_X = 64
PIXELS = TILE_SIDE * TILE_SIDE
CHUNK = 256
FIELDS = 9
REC_ROWS = 40
PIECES = (3, 3, 2, 2, 2, 2, 2, 2, 2)
PIECE_AT = tuple(sum(PIECES[:f]) for f in range(FIELDS + 1))

FOCAL = 3200.0
DILATION = 0.3
SH_ZERO = 0.28209479177387814
ALPHA_CAP = 0.99
LOG2E = 1.4426950408889634
DARK = -200.0


def project_kernel(params_ref, lists_ref, rec_ref, count_ref):
    def row(index):
        return params_ref[index : index + 1, :]

    mean_x, mean_y, mean_z = row(0), row(1), row(2)
    scales = [jnp.exp(row(3 + k)) for k in range(3)]
    quat = [row(6 + k) for k in range(4)]
    norm = jnp.sqrt(quat[0] * quat[0] + quat[1] * quat[1] + quat[2] * quat[2] + quat[3] * quat[3])
    qw, qx, qy, qz = [q / norm for q in quat]
    rotation = [
        [1.0 - 2.0 * (qy * qy + qz * qz), 2.0 * (qx * qy - qw * qz), 2.0 * (qx * qz + qw * qy)],
        [2.0 * (qx * qy + qw * qz), 1.0 - 2.0 * (qx * qx + qz * qz), 2.0 * (qy * qz - qw * qx)],
        [2.0 * (qx * qz - qw * qy), 2.0 * (qy * qz + qw * qx), 1.0 - 2.0 * (qx * qx + qy * qy)],
    ]
    inv_z = 1.0 / mean_z
    jac_a = FOCAL * inv_z
    jac_x = -FOCAL * mean_x * inv_z * inv_z
    jac_y = -FOCAL * mean_y * inv_z * inv_z
    first = [(jac_a * rotation[0][k] + jac_x * rotation[2][k]) * scales[k] for k in range(3)]
    second = [(jac_a * rotation[1][k] + jac_y * rotation[2][k]) * scales[k] for k in range(3)]
    cov_a = first[0] * first[0] + first[1] * first[1] + first[2] * first[2] + DILATION
    cov_b = first[0] * second[0] + first[1] * second[1] + first[2] * second[2]
    cov_c = second[0] * second[0] + second[1] * second[1] + second[2] * second[2] + DILATION
    determinant = cov_a * cov_c - cov_b * cov_b
    logit = row(10)
    log_opacity = -LOG2E * (jnp.maximum(-logit, 0.0) + jnp.log1p(jnp.exp(-jnp.abs(logit))))
    fields = [
        FOCAL * mean_x * inv_z + SCREEN_W / 2,
        FOCAL * mean_y * inv_z + SCREEN_H / 2,
        (-0.5 * LOG2E) * (cov_c / determinant),
        LOG2E * (cov_b / determinant),
        (-0.5 * LOG2E) * (cov_a / determinant),
        jnp.maximum(log_opacity, DARK),
    ] + [jnp.maximum(SH_ZERO * row(11 + k) + 0.5, 0.0) for k in range(3)]
    rec_ref[...] = jnp.zeros_like(rec_ref)
    for f, value in enumerate(fields):
        for q in range(4):
            rec_ref[4 * f + q : 4 * f + q + 1, :] = value[:, 128 * q : 128 * (q + 1)]
    live = (lists_ref[...] >= 0).astype(jnp.int32)
    count_ref[...] = jnp.broadcast_to(jnp.sum(live, axis=1, keepdims=True), count_ref.shape)


def pieces_of(value, count):
    found = []
    for _ in range(count):
        piece = value.astype(jnp.bfloat16)
        found.append(piece)
        value = value - piece.astype(jnp.float32)
    return found


def render_kernel(
    pair_bit, off_x, off_y, tids_ref, count_ref, mine_ref, other_ref, lists_ref,
    color_ref, trans_ref, sig_ref,
    table_ref, feat_ref, exp0_ref, exp1_ref, w0_ref, w1_ref, rgb_ref, acc_ref, through_ref,
):
    f32, bf16 = jnp.float32, jnp.bfloat16
    tiles = lists_ref.shape[0]
    half = mine_ref.shape[0] // REC_ROWS
    devices = 2 * half
    groups = tiles // 8
    me = lax.axis_index(("blk", "row"))
    my_bit = jnp.bitwise_and(jnp.right_shift(me, pair_bit), 1)

    for f in range(FIELDS):
        for q in range(4):
            for part, ref in enumerate((mine_ref, other_ref)):
                rows = ref[pl.ds(4 * f + q, half, stride=REC_ROWS), :]
                for p, piece in enumerate(pieces_of(rows, PIECES[f])):
                    at = (PIECE_AT[f] + p) * 2 * devices + (q // 2) * devices + part * half
                    table_ref[pl.ds(at, half), pl.ds(128 * (q % 2), 128)] = piece

    pixel = lax.broadcasted_iota(jnp.int32, (8, PIXELS), 1)
    which = lax.broadcasted_iota(jnp.int32, (8, PIXELS), 0)
    px = jnp.bitwise_and(pixel, TILE_SIDE - 1).astype(f32) - 7.5
    py = jnp.right_shift(pixel, 4).astype(f32) - 7.5
    feats = jnp.zeros((8, PIXELS), f32)
    for j, value in enumerate((px * px, px * py, py * py, px, py, jnp.ones_like(px))):
        feats = jnp.where(which == j, value, feats)
    feat_ref[...] = jnp.concatenate([feats, feats, feats, jnp.zeros_like(feats)], axis=0).astype(bf16)

    through_ref[...] = jnp.ones_like(through_ref)
    acc_ref[...] = jnp.zeros_like(acc_ref)
    sig_ref[...] = jnp.zeros_like(sig_ref)
    most = count_ref[0, 0]
    for t in range(1, tiles):
        most = jnp.maximum(most, count_ref[t, 0])

    def ids_of(t, c):
        return lists_ref[pl.ds(t, 1), pl.ds(pl.multiple_of(c * CHUNK, CHUNK), CHUNK)]

    def prepare(t, c):
        ids = ids_of(t, c)
        lane = jnp.bitwise_and(ids, 255)
        owner = jnp.right_shift(ids, 9)
        low = jnp.bitwise_and(owner, (1 << pair_bit) - 1)
        rank = jnp.left_shift(jnp.right_shift(owner, pair_bit + 1), pair_bit) + low
        part = jnp.bitwise_xor(jnp.bitwise_and(jnp.right_shift(owner, pair_bit), 1), my_bit)
        place = jnp.bitwise_and(jnp.right_shift(ids, 8), 1) * devices + part * half + rank
        place = jnp.where(ids >= 0, place, -1)
        onehot = (lax.broadcasted_iota(jnp.int32, (256, CHUNK), 0) == lane).astype(f32).astype(bf16)
        chosen = lax.broadcasted_iota(jnp.int32, (2 * devices, CHUNK), 0) == place

        def fetch(f):
            total = None
            for p in range(PIECE_AT[f], PIECE_AT[f + 1]):
                part = jnp.dot(
                    table_ref[p * 2 * devices : (p + 1) * 2 * devices, :], onehot, preferred_element_type=f32
                )
                total = part if total is None else total + part
            return jnp.sum(jnp.where(chosen, total, 0.0), axis=0, keepdims=True)

        u, v, ca, cb, cc, log_op, red, green, blue = [fetch(f) for f in range(FIELDS)]
        tid = tids_ref[t]
        center_x = (off_x + TILE_SIDE // 2 + TILE_SIDE * jnp.bitwise_and(tid, WIN_X - 1)).astype(f32)
        center_y = (off_y + TILE_SIDE // 2 + TILE_SIDE * jnp.right_shift(tid, 6)).astype(f32)
        du = u - center_x
        dv = v - center_y
        log_op = jnp.where(ids >= 0, log_op, DARK)
        terms = (
            ca,
            cb,
            cc,
            -2.0 * ca * du - cb * dv,
            -2.0 * cc * dv - cb * du,
            ca * du * du + cc * dv * dv + cb * du * dv + log_op,
        )
        row8 = lax.broadcasted_iota(jnp.int32, (8, CHUNK), 0)
        coef = jnp.zeros((8, CHUNK), f32)
        for j, value in enumerate(terms):
            coef = jnp.where(row8 == j, value, coef)
        p0, p1, p2 = [p.astype(f32) for p in pieces_of(coef, 3)]
        coefs = jnp.concatenate([p0, p1, p2, jnp.zeros_like(p0)], axis=0).astype(bf16)
        exponent = lax.dot_general(
            coefs, feat_ref[...], (((0,), (0,)), ((), ())), preferred_element_type=f32
        )
        at = pl.ds(pl.multiple_of(t * CHUNK, CHUNK), CHUNK)
        exp0_ref[at, :] = exponent[:, :128]
        exp1_ref[at, :] = exponent[:, 128:]
        rgb = jnp.zeros((8, CHUNK), f32)
        for j, value in enumerate((red, green, blue)):
            rgb = jnp.where(row8 == j, value, rgb)
        c0, c1 = pieces_of(rgb, 2)
        rgb_ref[pl.ds(pl.multiple_of(t * 16, 16), 16), :] = jnp.concatenate(
            [c0.astype(f32), c1.astype(f32)], axis=0
        ).astype(bf16)

    def blend(step, through):
        for j in range(8):
            k = step * 8 + j
            after = []
            for g in range(groups):
                for h, (e_ref, w_ref) in enumerate(((exp0_ref, w0_ref), (exp1_ref, w1_ref))):
                    at = pl.ds(g * 8 * CHUNK + k, 8, stride=CHUNK)
                    alpha = jnp.minimum(jnp.exp2(e_ref[at, :]), ALPHA_CAP)
                    before = through[2 * g + h]
                    w_ref[at, :] = before * alpha
                    after.append(before * (1.0 - alpha))
            through = tuple(after)
        return through

    def collect(t, c):
        ids = ids_of(t, c)
        at = pl.ds(pl.multiple_of(t * CHUNK, CHUNK), CHUNK)
        weight = jnp.concatenate([w0_ref[at, :], w1_ref[at, :]], axis=1)
        w_hi, w_lo = pieces_of(weight, 2)
        at16 = pl.ds(pl.multiple_of(t * 16, 16), 16)
        rgb = rgb_ref[at16, :]
        acc_ref[at16, :] += jnp.dot(rgb, w_hi, preferred_element_type=f32) + jnp.dot(
            rgb, w_lo, preferred_element_type=f32
        )
        ones = jnp.ones((16, PIXELS), bf16)
        nt = (((1,), (1,)), ((), ()))
        sums = lax.dot_general(ones, w_hi, nt, preferred_element_type=f32) + lax.dot_general(
            ones, w_lo, nt, preferred_element_type=f32
        )
        s0, s1 = pieces_of(sums[0:1, :], 2)
        rows = sig_ref.shape[0]
        hit = lax.broadcasted_iota(jnp.int32, (rows, CHUNK), 0) == jnp.right_shift(ids, 7)
        lanes = (
            lax.broadcasted_iota(jnp.int32, (128, CHUNK), 0) == jnp.bitwise_and(ids, 127)
        ).astype(f32).astype(bf16)
        left = jnp.concatenate(
            [jnp.where(hit, s.astype(f32), 0.0).astype(bf16) for s in (s0, s1)], axis=0
        )
        both = lax.dot_general(left, lanes, nt, preferred_element_type=f32)
        sig_ref[...] += both[:rows] + both[rows:]

    def chunk_body(c, carry):
        def prep_body(t, _):
            active = count_ref[t, 0] > c * CHUNK

            @pl.when(active)
            def _():
                prepare(t, c)

            @pl.when(jnp.logical_not(active))
            def _():
                at = pl.ds(pl.multiple_of(t * CHUNK, CHUNK), CHUNK)
                exp0_ref[at, :] = jnp.full((CHUNK, 128), DARK, f32)
                exp1_ref[at, :] = jnp.full((CHUNK, 128), DARK, f32)

            return 0

        lax.fori_loop(0, tiles, prep_body, 0)
        through = tuple(through_ref[8 * i : 8 * i + 8, :] for i in range(2 * groups))
        through = lax.fori_loop(0, CHUNK // 8, blend, through)
        for i in range(2 * groups):
            through_ref[8 * i : 8 * i + 8, :] = through[i]

        def collect_body(t, _):
            @pl.when(count_ref[t, 0] > c * CHUNK)
            def _():
                collect(t, c)

            return 0

        lax.fori_loop(0, tiles, collect_body, 0)
        return carry

    lax.fori_loop(0, (most + CHUNK - 1) // CHUNK, chunk_body, 0)

    for t in range(tiles):
        color_ref[t] = acc_ref[16 * t : 16 * t + 3, :] + acc_ref[16 * t + 8 : 16 * t + 11, :]
    for g in range(groups):
        for h in range(2):
            i = 2 * g + h
            trans_ref[8 * g : 8 * g + 8, 128 * h : 128 * (h + 1)] = through_ref[8 * i : 8 * i + 8, :]
    sig_ref[...] = sig_ref[...] * (1.0 / PIXELS)


def local(pair_bit, gauss_params, tile_ids, tile_lists):
    axes = ("blk", "row")
    devices = lax.axis_size(axes)
    tiles_here, list_len = tile_lists.shape
    half = devices // 2
    records, counts = pl.pallas_call(
        project_kernel,
        out_shape=(
            jax.ShapeDtypeStruct((REC_ROWS, 128), jnp.float32),
            jax.ShapeDtypeStruct((tiles_here, 128), jnp.int32),
        ),
    )(gauss_params, tile_lists)
    bit = 1 << pair_bit
    members = [[d for d in range(devices) if (d & bit) == part * bit] for part in range(2)]
    mine = lax.all_to_all(
        jnp.broadcast_to(records[None], (half, REC_ROWS, 128)), axes, 0, 0, axis_index_groups=members
    ).reshape(half * REC_ROWS, 128)
    other = lax.ppermute(mine, axes, [(d, d ^ bit) for d in range(devices)])

    tiles_total = tiles_here * devices
    win_y = tiles_total // WIN_X
    off_x = (SCREEN_W - WIN_X * TILE_SIDE) // 2
    off_y = (SCREEN_H - win_y * TILE_SIDE) // 2
    sig_rows = devices * gauss_params.shape[1] // 128
    vmem = pl.BlockSpec(memory_space=pltpu.VMEM)
    smem = pl.BlockSpec(memory_space=pltpu.SMEM)
    pixel_colors, transmittance, partial_sig = pl.pallas_call(
        functools.partial(render_kernel, pair_bit, off_x, off_y),
        out_shape=(
            jax.ShapeDtypeStruct((tiles_here, 3, PIXELS), jnp.float32),
            jax.ShapeDtypeStruct((tiles_here, PIXELS), jnp.float32),
            jax.ShapeDtypeStruct((sig_rows, 128), jnp.float32),
        ),
        in_specs=[smem, smem, vmem, vmem, vmem],
        out_specs=(vmem, vmem, vmem),
        scratch_shapes=[
            pltpu.VMEM((PIECE_AT[-1] * 2 * devices, 256), jnp.bfloat16),
            pltpu.VMEM((32, PIXELS), jnp.bfloat16),
            pltpu.VMEM((tiles_here * CHUNK, 128), jnp.float32),
            pltpu.VMEM((tiles_here * CHUNK, 128), jnp.float32),
            pltpu.VMEM((tiles_here * CHUNK, 128), jnp.float32),
            pltpu.VMEM((tiles_here * CHUNK, 128), jnp.float32),
            pltpu.VMEM((tiles_here * 16, CHUNK), jnp.bfloat16),
            pltpu.VMEM((tiles_here * 16, PIXELS), jnp.float32),
            pltpu.VMEM((tiles_here * 2, 128), jnp.float32),
        ],
        compiler_params=pltpu.CompilerParams(vmem_limit_bytes=48 * 2**20),
    )(tile_ids, counts, mine, other, tile_lists)
    swapped = lax.all_to_all(partial_sig.reshape(devices, -1, 128), axes, 0, 0)
    significance = jnp.sum(swapped, axis=0).reshape(-1)
    return (pixel_colors, transmittance, significance)


def pair_bit_of(mesh):
    flat = list(mesh.devices.flat)
    bit = 0
    while (2 << bit) <= len(flat):
        if getattr(flat[0], "coords", 0) == getattr(flat[1 << bit], "coords", 1):
            return bit
        bit += 1
    return 0


def solution(mesh):
    return jax.shard_map(
        functools.partial(local, pair_bit_of(mesh)),
        mesh=mesh,
        in_specs=(P(None, ("blk", "row")), P(("blk", "row")), P(("blk", "row"), None)),
        out_specs=(P(("blk", "row"), None, None), P(("blk", "row"), None), P(("blk", "row"))),
        check_vma=False,
    )
```

time: 569 us -> 95.9 us (0.17)
  other arithmetic: 220 us -> 0.62 us
  waiting for transfers between devices: 147 us -> 8.49 us
  local copies, waits for them, and re-layouts: 86.9 us -> 1.4 us
  Pallas kernels: 0 us -> 59.6 us
  blocking collectives: 78.8 us -> 20.2 us
  between operations: 14.2 us -> 0.66 us
  loops' own time: 12.3 us -> 0 us
  matrix products: 6 us -> 0 us
    unnamed x2 -> x0, waiting for transfers between devices: 147 us -> none
    scatter-add x1 -> x0, other arithmetic: 102 us -> none  [local(): jax.ops.segment_sum(flat_weights, seg_ids, num_segments=row_count + 1)]
    all_gather x1 -> x0, blocking collectives: 78.8 us -> none  [local(): lax.all_gather(gauss_params, ('blk', 'row'), axis=1, tiled=True)]
    gather x2 -> x0, local copies, waits for them, and re-layouts: 63 us -> none  [place_records(): fetched = jnp.take(piece_rec, jnp.clip(flat_ids, 0, width - 1), axis=1)]
    pallas_call x0 -> x2, Pallas kernels: none -> 59.6 us  [the longest x1 58.1 us: local(): pl.pallas_call(functools.partial(render_kernel, pair_bit, off_x, off_y),...]
    reduce_sum x10 -> x1, other arithmetic: 59.3 us -> 0.62 us  [local(): significance = jnp.sum(swapped, axis=0).reshape(-1)]
    another operation x18 -> x0, other arithmetic: 35.5 us -> none
    all_to_all x0 -> x1, blocking collectives: none -> 20.2 us  [local(): lax.all_to_all(jnp.broadcast_to(records[None], (half, REC_ROWS, 128)), ax...]
  transfers between devices with their start and end apart: 1 -> 2, of which waited for: 1 -> 2; matrix products, arithmetic and copies ran while one was open for 0% -> 1% of each run, Pallas kernels for 0% -> 0%
where the time goes in v1:
time: 95.9 us; the launch traced here: 96 us
  Pallas kernels  59.6 us (62%)
  blocking collectives  20.2 us (21%)
  waiting for transfers between devices  8.49 us (9%)
  starting transfers between devices  4.95 us (5%)
  local copies, waits for them, and re-layouts  1.4 us (1%)
    pallas_call x1, Pallas kernels, local(): pl.pallas_call(functools.partial(render_kernel, pair_bit, off_x, off_y),...  58.1 us
    all_to_all x1, blocking collectives, local(): lax.all_to_all(jnp.broadcast_to(records[None], (half, REC_ROWS, 128)), ax...  20.2 us
    all_to_all x1, waiting for transfers between devices, local(): swapped = lax.all_to_all(partial_sig.reshape(devices, -1, 128), axes, 0, 0)  6.87 us
    all_to_all x1, starting transfers between devices, local(): swapped = lax.all_to_all(partial_sig.reshape(devices, -1, 128), axes, 0, 0)  4.95 us
  transfers between devices with their start and end apart: 2, of which 2 were waited for; matrix products, arithmetic and copies ran while one was open for 1% of the time, Pallas kernels for 0%

profile of v1, /device:TPU:0, one launch (start us, length us, event | category | flops | bytes accessed | tf_op | source)
XLA Modules:
  0.0 96.0 jit_solution(2890127543076064305)
XLA Ops:
  0.6 1.5 %shard_map.58 = (f32[40,128]{1,0:T(8,128)}, s32[16,128]{1,0:T(8,128)}) custom-call(f32[14,512]{1,0:T(8,128)} %params_ref.1, s32[16,1024]{1,0:T(8,128)} %lists_ref.3), custom_call_target="tpu_custom_call" | custom-call | tf_op jit(solution)/shard_map/pallas_call | solution.py:265
  2.2 0.7 broadcast_in_dim.2
  2.9 0.0 copy-start
  2.9 0.0 copy-start.1
  3.0 20.2 %all_to_all.10 = f32[16,40,128]{2,1,0:T(8,128)S(1)} all-to-all(f32[16,40,128]{2,1,0:T(8,128)S(1)} %broadcast_in_dim.2), channel_id=1, replica_groups={{0,1,2,3,8,9,10,11,16,17,18,19,24,25,26,27},{4,5,6,7,12,13,14,15,20,21,..., dimensions={0} | all-to-all | bytes 655360 | tf_op jit(solution)/shard_map/all_to_all | solution.py:274
  23.2 0.0 copy-start.2
  23.2 0.0 collective-permute-start
  23.2 1.6 %collective-permute-done.other_ref = f32[640,128]{1,0:T(8,128)S(1)} collective-permute-done((f32[640,128]{1,0:T(8,128)S(1)}, f32[640,128]{1,0:T(8,128)S(1)}, u32[]{:S(2)}, u32[]{:S(2)}) %collective-permute-start) | collective-permute-done | bytes 327712 | tf_op jit(solution)/shard_map/ppermute | solution.py:277
  24.8 0.0 copy-done
  24.8 0.0 copy-done.1
  24.8 0.0 copy-done.2
  24.8 58.1 %shard_map.59 = (f32[16,3,256]{2,1,0:T(4,128)S(1)}, f32[16,256]{1,0:T(8,128)}, f32[128,128]{1,0:T(8,128)}) custom-call(s32[16]{0:T(128)S(1)} %copy-done.2, s32[16,128]{1,0:T(8,128)S(1)} %copy-done.1, f32[640,128]{1,0:T(8,128)S(1)} %bitcast.4, f32[640,128]{1,0:T(8,128)S(1)} %collective-permute-done.other_ref, s32[16,1024]{1,0:T(8,128)S(1)} %copy-done), custom_call_target="tpu_custom_call" | custom-call | tf_op jit(solution)/shard_map/pallas_call | solution.py:286
  82.9 4.9 %all-to-all-start.1 = ((f32[32,4,128]{2,1,0:T(4,128)}), f32[32,4,128]{2,1,0:T(4,128)S(1)}, u32[]{:S(2)}, u32[]{:S(2)}) async-start(f32[32,4,128]{2,1,0:T(4,128)} %bitcast.1), calls=%async_computation.1 | async-start | bytes 131072 | tf_op jit(solution)/shard_map/all_to_all | solution.py:308
  87.9 0.6 copy.6
  88.5 6.9 %all-to-all-done.1 = f32[32,4,128]{2,1,0:T(4,128)S(1)} async-done(((f32[32,4,128]{2,1,0:T(4,128)}), f32[32,4,128]{2,1,0:T(4,128)S(1)}, u32[]{:S(2)}, u32[]{:S(2)}) %all-to-all-start.1) | async-done | bytes 65568 | tf_op jit(solution)/shard_map/all_to_all | solution.py:308
  95.4 0.6 reduce_sum.9
Async XLA Ops:
  2.9 21.9 %copy-start = (s32[16,1024]{1,0:T(8,128)S(1)}, s32[16,1024]{1,0:T(8,128)}, u32[]{:S(2)}) copy-start(s32[16,1024]{1,0:T(8,128)} %lists_ref.3) | copy-start | bytes 196612
  2.9 21.9 %copy-start.1 = (s32[16,128]{1,0:T(8,128)S(1)}, s32[16,128]{1,0:T(8,128)}, u32[]{:S(2)}) copy-start(s32[16,128]{1,0:T(8,128)} %get-tuple-element.8.count_ref) | copy-start | bytes 24580
  23.2 1.6 %copy-start.2 = (s32[16]{0:T(128)S(1)}, s32[16]{0:T(128)}, u32[]{:S(2)}) copy-start(s32[16]{0:T(128)} %tids_ref.1) | copy-start | bytes 196
  23.2 1.6 %collective-permute-start = (f32[640,128]{1,0:T(8,128)S(1)}, f32[640,128]{1,0:T(8,128)S(1)}, u32[]{:S(2)}, u32[]{:S(2)}) collective-permute-start(f32[640,128]{1,0:T(8,128)S(1)} %bitcast.3), channel_id=1, source_target_pairs={{0,4},{1,5},{2,6},{3,7},{4,0},{5,1},{6,2},{7,3},{8,12},{9,13},{10,... | collective-permute-start | bytes 983048 | tf_op jit(solution)/shard_map/ppermute | solution.py:277
  82.9 12.5 %all-to-all-start.1 = ((f32[32,4,128]{2,1,0:T(4,128)}), f32[32,4,128]{2,1,0:T(4,128)S(1)}, u32[]{:S(2)}, u32[]{:S(2)}) async-start(f32[32,4,128]{2,1,0:T(4,128)} %bitcast.1), calls=%async_computation.1 | async-start | bytes 131072 | tf_op jit(solution)/shard_map/all_to_all | solution.py:308

commit v2 on v1

--- a/solution.py
+++ b/solution.py
@@ -13,6 +13,8 @@
 WIN_X = 64
 PIXELS = TILE_SIDE * TILE_SIDE
 CHUNK = 256
+STRIDE = CHUNK + 8
+UNROLL = 8
 FIELDS = 9
 REC_ROWS = 40
 PIECES = (3, 3, 2, 2, 2, 2, 2, 2, 2)
@@ -81,6 +83,7 @@
     pair_bit, off_x, off_y, tids_ref, count_ref, mine_ref, other_ref, lists_ref,
     color_ref, trans_ref, sig_ref,
     table_ref, feat_ref, exp0_ref, exp1_ref, w0_ref, w1_ref, rgb_ref, acc_ref, through_ref,
+    ids_ref, coef_ref, slot_ref,
 ):
     f32, bf16 = jnp.float32, jnp.bfloat16
     tiles = lists_ref.shape[0]
@@ -115,31 +118,35 @@
         most = jnp.maximum(most, count_ref[t, 0])
 
     def ids_of(t, c):
-        return lists_ref[pl.ds(t, 1), pl.ds(pl.multiple_of(c * CHUNK, CHUNK), CHUNK)]
+        return ids_ref[pl.ds(t, 1), pl.ds(pl.multiple_of(c * CHUNK, CHUNK), CHUNK)]
+
+    def slot(t):
+        return pl.ds(pl.multiple_of(t * STRIDE, 8), CHUNK)
+
+    def one_hot(rows, index):
+        iota = lax.broadcasted_iota(jnp.int32, (rows, index.shape[1]), 0)
+        return (iota == index).astype(f32).astype(bf16)
 
     def prepare(t, c):
         ids = ids_of(t, c)
-        lane = jnp.bitwise_and(ids, 255)
         owner = jnp.right_shift(ids, 9)
         low = jnp.bitwise_and(owner, (1 << pair_bit) - 1)
         rank = jnp.left_shift(jnp.right_shift(owner, pair_bit + 1), pair_bit) + low
         part = jnp.bitwise_xor(jnp.bitwise_and(jnp.right_shift(owner, pair_bit), 1), my_bit)
         place = jnp.bitwise_and(jnp.right_shift(ids, 8), 1) * devices + part * half + rank
         place = jnp.where(ids >= 0, place, -1)
-        onehot = (lax.broadcasted_iota(jnp.int32, (256, CHUNK), 0) == lane).astype(f32).astype(bf16)
         chosen = lax.broadcasted_iota(jnp.int32, (2 * devices, CHUNK), 0) == place
+        looked = jnp.dot(table_ref[...], one_hot(256, jnp.bitwise_and(ids, 255)), preferred_element_type=f32)
 
         def fetch(f):
             total = None
             for p in range(PIECE_AT[f], PIECE_AT[f + 1]):
-                part = jnp.dot(
-                    table_ref[p * 2 * devices : (p + 1) * 2 * devices, :], onehot, preferred_element_type=f32
-                )
-                total = part if total is None else total + part
+                piece = looked[p * 2 * devices : (p + 1) * 2 * devices]
+                total = piece if total is None else total + piece
             return jnp.sum(jnp.where(chosen, total, 0.0), axis=0, keepdims=True)
 
         u, v, ca, cb, cc, log_op, red, green, blue = [fetch(f) for f in range(FIELDS)]
-        tid = tids_ref[t]
+        tid = tids_ref[jnp.minimum(t, tiles - 1)]
         center_x = (off_x + TILE_SIDE // 2 + TILE_SIDE * jnp.bitwise_and(tid, WIN_X - 1)).astype(f32)
         center_y = (off_y + TILE_SIDE // 2 + TILE_SIDE * jnp.right_shift(tid, 6)).astype(f32)
         du = u - center_x
@@ -158,13 +165,9 @@
         for j, value in enumerate(terms):
             coef = jnp.where(row8 == j, value, coef)
         p0, p1, p2 = [p.astype(f32) for p in pieces_of(coef, 3)]
-        coefs = jnp.concatenate([p0, p1, p2, jnp.zeros_like(p0)], axis=0).astype(bf16)
-        exponent = lax.dot_general(
-            coefs, feat_ref[...], (((0,), (0,)), ((), ())), preferred_element_type=f32
-        )
-        at = pl.ds(pl.multiple_of(t * CHUNK, CHUNK), CHUNK)
-        exp0_ref[at, :] = exponent[:, :128]
-        exp1_ref[at, :] = exponent[:, 128:]
+        coef_ref[pl.ds(pl.multiple_of(t * 32, 32), 32), :] = jnp.concatenate(
+            [p0, p1, p2, jnp.zeros_like(p0)], axis=0
+        ).astype(bf16)
         rgb = jnp.zeros((8, CHUNK), f32)
         for j, value in enumerate((red, green, blue)):
             rgb = jnp.where(row8 == j, value, rgb)
@@ -173,13 +176,21 @@
             [c0.astype(f32), c1.astype(f32)], axis=0
         ).astype(bf16)
 
+    def exponents(t):
+        exponent = lax.dot_general(
+            coef_ref[pl.ds(pl.multiple_of(t * 32, 32), 32), :], feat_ref[...],
+            (((0,), (0,)), ((), ())), preferred_element_type=f32,
+        )
+        exp0_ref[slot(t), :] = exponent[:, :128]
+        exp1_ref[slot(t), :] = exponent[:, 128:]
+
     def blend(step, through):
         for j in range(8):
             k = step * 8 + j
             after = []
             for g in range(groups):
                 for h, (e_ref, w_ref) in enumerate(((exp0_ref, w0_ref), (exp1_ref, w1_ref))):
-                    at = pl.ds(g * 8 * CHUNK + k, 8, stride=CHUNK)
+                    at = pl.ds(g * 8 * STRIDE + k, 8, stride=STRIDE)
                     alpha = jnp.minimum(jnp.exp2(e_ref[at, :]), ALPHA_CAP)
                     before = through[2 * g + h]
                     w_ref[at, :] = before * alpha
@@ -187,65 +198,80 @@
             through = tuple(after)
         return through
 
-    def collect(t, c):
-        ids = ids_of(t, c)
-        at = pl.ds(pl.multiple_of(t * CHUNK, CHUNK), CHUNK)
-        weight = jnp.concatenate([w0_ref[at, :], w1_ref[at, :]], axis=1)
-        w_hi, w_lo = pieces_of(weight, 2)
-        at16 = pl.ds(pl.multiple_of(t * 16, 16), 16)
-        rgb = rgb_ref[at16, :]
-        acc_ref[at16, :] += jnp.dot(rgb, w_hi, preferred_element_type=f32) + jnp.dot(
-            rgb, w_lo, preferred_element_type=f32
+    def collect(slots, c):
+        left, right = [], []
+        for t in slots:
+            ids = ids_of(t, c)
+            w0, w1 = w0_ref[slot(t), :], w1_ref[slot(t), :]
+            high, low = pieces_of(jnp.concatenate([w0, w1], axis=1), 2)
+            at16 = pl.ds(pl.multiple_of(t * 16, 16), 16)
+            rgb = rgb_ref[at16, :]
+            acc_ref[at16, :] += jnp.dot(rgb, high, preferred_element_type=f32) + jnp.dot(
+                rgb, low, preferred_element_type=f32
+            )
+            sums = jnp.sum(w0 + w1, axis=1, keepdims=True)
+            inner = jnp.bitwise_and(ids, 127)
+            columns = jnp.concatenate(
+                [
+                    jnp.broadcast_to(inner[:, 128 * i : 128 * (i + 1)], (128, 128)).T
+                    for i in range(CHUNK // 128)
+                ],
+                axis=0,
+            )
+            spread = jnp.where(lax.broadcasted_iota(jnp.int32, (CHUNK, 128), 1) == columns, sums, 0.0)
+            right.append(jnp.concatenate(pieces_of(spread, 2), axis=1))
+            left.append(one_hot(sig_ref.shape[0], jnp.right_shift(ids, 7)))
+        both = jnp.dot(
+            jnp.concatenate(left, axis=1), jnp.concatenate(right, axis=0), preferred_element_type=f32
         )
-        ones = jnp.ones((16, PIXELS), bf16)
-        nt = (((1,), (1,)), ((), ()))
-        sums = lax.dot_general(ones, w_hi, nt, preferred_element_type=f32) + lax.dot_general(
-            ones, w_lo, nt, preferred_element_type=f32
-        )
-        s0, s1 = pieces_of(sums[0:1, :], 2)
-        rows = sig_ref.shape[0]
-        hit = lax.broadcasted_iota(jnp.int32, (rows, CHUNK), 0) == jnp.right_shift(ids, 7)
-        lanes = (
-            lax.broadcasted_iota(jnp.int32, (128, CHUNK), 0) == jnp.bitwise_and(ids, 127)
-        ).astype(f32).astype(bf16)
-        left = jnp.concatenate(
-            [jnp.where(hit, s.astype(f32), 0.0).astype(bf16) for s in (s0, s1)], axis=0
-        )
-        both = lax.dot_general(left, lanes, nt, preferred_element_type=f32)
-        sig_ref[...] += both[:rows] + both[rows:]
+        sig_ref[...] += both[:, :128] + both[:, 128:]
 
     def chunk_body(c, carry):
-        def prep_body(t, _):
-            active = count_ref[t, 0] > c * CHUNK
-
-            @pl.when(active)
+        found = jnp.int32(0)
+        for t in range(tiles):
+            slot_ref[found] = t
+            found += (count_ref[t, 0] > c * CHUNK).astype(jnp.int32)
+        for i in range(UNROLL):
+            slot_ref[found + i] = tiles
+        rounds = (found + UNROLL - 1) // UNROLL
+
+        def prep_body(i, _):
+            for j in range(UNROLL):
+                prepare(slot_ref[i * UNROLL + j], c)
+            return 0
+
+        def exponent_body(i, _):
+            for j in range(UNROLL):
+                exponents(slot_ref[i * UNROLL + j])
+            return 0
+
+        def dark_body(t, _):
+            @pl.when(count_ref[t, 0] <= c * CHUNK)
             def _():
-                prepare(t, c)
-
-            @pl.when(jnp.logical_not(active))
-            def _():
-                at = pl.ds(pl.multiple_of(t * CHUNK, CHUNK), CHUNK)
-                exp0_ref[at, :] = jnp.full((CHUNK, 128), DARK, f32)
-                exp1_ref[at, :] = jnp.full((CHUNK, 128), DARK, f32)
+                exp0_ref[slot(t), :] = jnp.full((CHUNK, 128), DARK, f32)
+                exp1_ref[slot(t), :] = jnp.full((CHUNK, 128), DARK, f32)
 
             return 0
 
-        lax.fori_loop(0, tiles, prep_body, 0)
+        lax.fori_loop(0, tiles, dark_body, 0)
+        lax.fori_loop(0, rounds, prep_body, 0)
+        lax.fori_loop(0, rounds, exponent_body, 0)
         through = tuple(through_ref[8 * i : 8 * i + 8, :] for i in range(2 * groups))
         through = lax.fori_loop(0, CHUNK // 8, blend, through)
         for i in range(2 * groups):
             through_ref[8 * i : 8 * i + 8, :] = through[i]
 
-        def collect_body(t, _):
-            @pl.when(count_ref[t, 0] > c * CHUNK)
-            def _():
-                collect(t, c)
-
+        def collect_body(i, _):
+            collect([slot_ref[i * UNROLL + j] for j in range(UNROLL)], c)
             return 0
 
-        lax.fori_loop(0, tiles, collect_body, 0)
+        lax.fori_loop(0, rounds, collect_body, 0)
         return carry
 
+    ids_ref[pl.ds(0, tiles), :] = lists_ref[...]
+    ids_ref[pl.ds(tiles, 8), :] = jnp.full((8, lists_ref.shape[1]), -1, jnp.int32)
+    w0_ref[slot(tiles), :] = jnp.zeros((CHUNK, 128), f32)
+    w1_ref[slot(tiles), :] = jnp.zeros((CHUNK, 128), f32)
     lax.fori_loop(0, (most + CHUNK - 1) // CHUNK, chunk_body, 0)
 
     for t in range(tiles):
@@ -295,13 +321,16 @@
         scratch_shapes=[
             pltpu.VMEM((PIECE_AT[-1] * 2 * devices, 256), jnp.bfloat16),
             pltpu.VMEM((32, PIXELS), jnp.bfloat16),
-            pltpu.VMEM((tiles_here * CHUNK, 128), jnp.float32),
-            pltpu.VMEM((tiles_here * CHUNK, 128), jnp.float32),
-            pltpu.VMEM((tiles_here * CHUNK, 128), jnp.float32),
-            pltpu.VMEM((tiles_here * CHUNK, 128), jnp.float32),
-            pltpu.VMEM((tiles_here * 16, CHUNK), jnp.bfloat16),
-            pltpu.VMEM((tiles_here * 16, PIXELS), jnp.float32),
+            pltpu.VMEM(((tiles_here + 1) * STRIDE, 128), jnp.float32),
+            pltpu.VMEM(((tiles_here + 1) * STRIDE, 128), jnp.float32),
+            pltpu.VMEM(((tiles_here + 1) * STRIDE, 128), jnp.float32),
+            pltpu.VMEM(((tiles_here + 1) * STRIDE, 128), jnp.float32),
+            pltpu.VMEM(((tiles_here + 1) * 16, CHUNK), jnp.bfloat16),
+            pltpu.VMEM(((tiles_here + 1) * 16, PIXELS), jnp.float32),
             pltpu.VMEM((tiles_here * 2, 128), jnp.float32),
+            pltpu.VMEM((tiles_here + 8, list_len), jnp.int32),
+            pltpu.VMEM(((tiles_here + 1) * 32, CHUNK), jnp.bfloat16),
+            pltpu.SMEM((tiles_here + UNROLL,), jnp.int32),
         ],
         compiler_params=pltpu.CompilerParams(vmem_limit_bytes=48 * 2**20),
     )(tile_ids, counts, mine, other, tile_lists)

time: 95.9 us -> 57.7 us (0.60)
  Pallas kernels: 59.6 us -> 23.4 us
  starting transfers between devices: 4.95 us -> 2.57 us
    pallas_call x1, Pallas kernels: 58.1 us -> 21.8 us  [local(): pl.pallas_call(functools.partial(render_kernel, pair_bit, off_x, off_y),...]
    all_to_all x1, starting transfers between devices: 4.95 us -> 2.57 us  [local(): swapped = lax.all_to_all(partial_sig.reshape(devices, -1, 128), axes, 0, 0)]
where the time goes in v2:
time: 57.7 us; the launch traced here: 57.3 us
  Pallas kernels  23.4 us (41%)
  blocking collectives  20.2 us (35%)
  waiting for transfers between devices  8.49 us (15%)
  starting transfers between devices  2.57 us (4%)
  local copies, waits for them, and re-layouts  1.4 us (2%)
  between operations  0.66 us (1%)
  other arithmetic  0.62 us (1%)
    pallas_call x1, Pallas kernels, local(): pl.pallas_call(functools.partial(render_kernel, pair_bit, off_x, off_y),...  21.8 us
    all_to_all x1, blocking collectives, local(): lax.all_to_all(jnp.broadcast_to(records[None], (half, REC_ROWS, 128)), ax...  20.2 us
    all_to_all x1, waiting for transfers between devices, local(): swapped = lax.all_to_all(partial_sig.reshape(devices, -1, 128), axes, 0, 0)  6.87 us
    all_to_all x1, starting transfers between devices, local(): swapped = lax.all_to_all(partial_sig.reshape(devices, -1, 128), axes, 0, 0)  2.57 us
    ppermute x1, waiting for transfers between devices, local(): other = lax.ppermute(mine, axes, [(d, d ^ bit) for d in range(devices)])  1.63 us
    pallas_call x1, Pallas kernels, local(): pl.pallas_call(project_kernel, out_shape=(jax.ShapeDtypeStruct((REC_ROWS,...  1.55 us
  transfers between devices with their start and end apart: 2, of which 2 were waited for; matrix products, arithmetic and copies ran while one was open for 1% of the time, Pallas kernels for 0%

profile of v2, /device:TPU:0, one launch (start us, length us, event | category | flops | bytes accessed | tf_op | source)
XLA Modules:
  0.0 57.3 jit_solution(234280978181562870)
XLA Ops:
  0.6 1.5 %shard_map.58 = (f32[40,128]{1,0:T(8,128)}, s32[16,128]{1,0:T(8,128)}) custom-call(f32[14,512]{1,0:T(8,128)} %params_ref.1, s32[16,1024]{1,0:T(8,128)} %lists_ref.3), custom_call_target="tpu_custom_call" | custom-call | tf_op jit(solution)/shard_map/pallas_call | solution.py:291
  2.2 0.7 %broadcast_in_dim.2 = f32[16,40,128]{2,1,0:T(8,128)S(1)} broadcast(f32[40,128]{1,0:T(8,128)} %get-tuple-element.9), dimensions={1,2} | broadcast | bytes 348160 | tf_op jit(solution)/shard_map/broadcast_in_dim | solution.py:301
  2.9 0.0 copy-start
  2.9 0.0 copy-start.1
  3.0 20.2 %all_to_all.10 = f32[16,40,128]{2,1,0:T(8,128)S(1)} all-to-all(f32[16,40,128]{2,1,0:T(8,128)S(1)} %broadcast_in_dim.2), channel_id=1, replica_groups={{0,1,2,3,8,9,10,11,16,17,18,19,24,25,26,27},{4,5,6,7,12,13,14,15,20,21,..., dimensions={0} | all-to-all | bytes 655360 | tf_op jit(solution)/shard_map/all_to_all | solution.py:300
  23.2 0.0 copy-start.2
  23.2 0.0 collective-permute-start
  23.2 1.6 %collective-permute-done.other_ref = f32[640,128]{1,0:T(8,128)S(1)} collective-permute-done((f32[640,128]{1,0:T(8,128)S(1)}, f32[640,128]{1,0:T(8,128)S(1)}, u32[]{:S(2)}, u32[]{:S(2)}) %collective-permute-start) | collective-permute-done | bytes 327712 | tf_op jit(solution)/shard_map/ppermute | solution.py:303
  24.8 0.0 copy-done
  24.8 0.0 copy-done.1
  24.8 0.0 copy-done.2
  24.8 21.8 %shard_map.59 = (f32[16,3,256]{2,1,0:T(4,128)S(1)}, f32[16,256]{1,0:T(8,128)}, f32[128,128]{1,0:T(8,128)}) custom-call(s32[16]{0:T(128)S(1)} %copy-done.2, s32[16,128]{1,0:T(8,128)S(1)} %copy-done.1, f32[640,128]{1,0:T(8,128)S(1)} %bitcast.4, f32[640,128]{1,0:T(8,128)S(1)} %collective-permute-done.other_ref, s32[16,1024]{1,0:T(8,128)S(1)} %copy-done), custom_call_target="tpu_custom_call" | custom-call | tf_op jit(solution)/shard_map/pallas_call | solution.py:312
  46.6 2.6 %all-to-all-start.1 = ((f32[32,4,128]{2,1,0:T(4,128)}), f32[32,4,128]{2,1,0:T(4,128)S(1)}, u32[]{:S(2)}, u32[]{:S(2)}) async-start(f32[32,4,128]{2,1,0:T(4,128)} %bitcast.1), calls=%async_computation.1 | async-start | bytes 131072 | tf_op jit(solution)/shard_map/all_to_all | solution.py:337
  49.2 0.6 %copy.6 = f32[16,3,256]{2,0,1:T(8,128)} copy(f32[16,3,256]{2,1,0:T(4,128)S(1)} %get-tuple-element.13) | data formatting | bytes 98304
  49.8 6.9 %all-to-all-done.1 = f32[32,4,128]{2,1,0:T(4,128)S(1)} async-done(((f32[32,4,128]{2,1,0:T(4,128)}), f32[32,4,128]{2,1,0:T(4,128)S(1)}, u32[]{:S(2)}, u32[]{:S(2)}) %all-to-all-start.1) | async-done | bytes 65568 | tf_op jit(solution)/shard_map/all_to_all | solution.py:337
  56.7 0.6 %reduce_sum.9 = f32[4,128]{1,0:T(4,128)} reduce(f32[32,4,128]{2,1,0:T(4,128)S(1)} %all-to-all-done.1, f32[]{:T(128)} %constant.0.clone.1), dimensions={0}, to_apply=%region_0.0 | reduce | flops 15872 | bytes 67588 | tf_op jit(solution)/shard_map/reduce_sum | solution.py:338
Async XLA Ops:
  2.9 21.9 %copy-start = (s32[16,1024]{1,0:T(8,128)S(1)}, s32[16,1024]{1,0:T(8,128)}, u32[]{:S(2)}) copy-start(s32[16,1024]{1,0:T(8,128)} %lists_ref.3) | copy-start | bytes 196612
  2.9 21.9 %copy-start.1 = (s32[16,128]{1,0:T(8,128)S(1)}, s32[16,128]{1,0:T(8,128)}, u32[]{:S(2)}) copy-start(s32[16,128]{1,0:T(8,128)} %get-tuple-element.8.count_ref) | copy-start | bytes 24580
  23.2 1.6 %copy-start.2 = (s32[16]{0:T(128)S(1)}, s32[16]{0:T(128)}, u32[]{:S(2)}) copy-start(s32[16]{0:T(128)} %tids_ref.1) | copy-start | bytes 196
  23.2 1.6 %collective-permute-start = (f32[640,128]{1,0:T(8,128)S(1)}, f32[640,128]{1,0:T(8,128)S(1)}, u32[]{:S(2)}, u32[]{:S(2)}) collective-permute-start(f32[640,128]{1,0:T(8,128)S(1)} %bitcast.3), channel_id=1, source_target_pairs={{0,4},{1,5},{2,6},{3,7},{4,0},{5,1},{6,2},{7,3},{8,12},{9,13},{10,... | collective-permute-start | bytes 983048 | tf_op jit(solution)/shard_map/ppermute | solution.py:303
  46.6 10.1 %all-to-all-start.1 = ((f32[32,4,128]{2,1,0:T(4,128)}), f32[32,4,128]{2,1,0:T(4,128)S(1)}, u32[]{:S(2)}, u32[]{:S(2)}) async-start(f32[32,4,128]{2,1,0:T(4,128)} %bitcast.1), calls=%async_computation.1 | async-start | bytes 131072 | tf_op jit(solution)/shard_map/all_to_all | solution.py:337

commit v3 on v1

v3 whole, which is shorter than its diff:
```python
import functools

import jax
import jax.numpy as jnp
from jax import lax
from jax.experimental import pallas as pl
from jax.experimental.pallas import tpu as pltpu
from jax.sharding import PartitionSpec as P

TILE_SIDE = 16
SCREEN_W = 3840
SCREEN_H = 2160
WIN_X = 64
PIXELS = TILE_SIDE * TILE_SIDE
BLOCK = 128
UNROLL = 8
FIELDS = 9
REC_ROWS = 40
LOOKED = 2
PIECES = ((0, 0) + (2,) * 7)
PIECE_AT = tuple(sum(PIECES[:f]) for f in range(FIELDS + 1))
AXES = ("blk", "row")

FOCAL = 3200.0
DILATION = 0.3
SH_ZERO = 0.28209479177387814
ALPHA_CAP = 0.99
LOG2E = 1.4426950408889634
DARK = -200.0


def project_kernel(params_ref, lists_ref, rec_ref, count_ref):
    def row(index):
        return params_ref[index : index + 1, :]

    mean_x, mean_y, mean_z = row(0), row(1), row(2)
    scales = [jnp.exp(row(3 + k)) for k in range(3)]
    quat = [row(6 + k) for k in range(4)]
    norm = jnp.sqrt(quat[0] * quat[0] + quat[1] * quat[1] + quat[2] * quat[2] + quat[3] * quat[3])
    qw, qx, qy, qz = [q / norm for q in quat]
    rotation = [
        [1.0 - 2.0 * (qy * qy + qz * qz), 2.0 * (qx * qy - qw * qz), 2.0 * (qx * qz + qw * qy)],
        [2.0 * (qx * qy + qw * qz), 1.0 - 2.0 * (qx * qx + qz * qz), 2.0 * (qy * qz - qw * qx)],
        [2.0 * (qx * qz - qw * qy), 2.0 * (qy * qz + qw * qx), 1.0 - 2.0 * (qx * qx + qy * qy)],
    ]
    inv_z = 1.0 / mean_z
    jac_a = FOCAL * inv_z
    jac_x = -FOCAL * mean_x * inv_z * inv_z
    jac_y = -FOCAL * mean_y * inv_z * inv_z
    first = [(jac_a * rotation[0][k] + jac_x * rotation[2][k]) * scales[k] for k in range(3)]
    second = [(jac_a * rotation[1][k] + jac_y * rotation[2][k]) * scales[k] for k in range(3)]
    cov_a = first[0] * first[0] + first[1] * first[1] + first[2] * first[2] + DILATION
    cov_b = first[0] * second[0] + first[1] * second[1] + first[2] * second[2]
    cov_c = second[0] * second[0] + second[1] * second[1] + second[2] * second[2] + DILATION
    determinant = cov_a * cov_c - cov_b * cov_b
    logit = row(10)
    log_opacity = -LOG2E * (jnp.maximum(-logit, 0.0) + jnp.log1p(jnp.exp(-jnp.abs(logit))))
    fields = [
        FOCAL * mean_x * inv_z + SCREEN_W / 2,
        FOCAL * mean_y * inv_z + SCREEN_H / 2,
        (-0.5 * LOG2E) * (cov_c / determinant),
        LOG2E * (cov_b / determinant),
        (-0.5 * LOG2E) * (cov_a / determinant),
        jnp.maximum(log_opacity, DARK),
    ] + [jnp.maximum(SH_ZERO * row(11 + k) + 0.5, 0.0) for k in range(3)]
    rec_ref[...] = jnp.zeros_like(rec_ref)
    for f, value in enumerate(fields):
        for q in range(4):
            rec_ref[4 * f + q : 4 * f + q + 1, :] = value[:, 128 * q : 128 * (q + 1)]
    live = (lists_ref[...] >= 0).astype(jnp.int32)
    count_ref[...] = jnp.broadcast_to(jnp.sum(live, axis=1, keepdims=True), count_ref.shape)


def pieces_of(value, count):
    found = []
    for _ in range(count):
        piece = value.astype(jnp.bfloat16)
        found.append(piece)
        value = value - piece.astype(jnp.float32)
    return found


def bit_of(value, bit):
    return jnp.bitwise_and(jnp.right_shift(value, bit), 1)


def render_kernel(
    off_x, off_y, bits, tids_ref, count_ref, mine_ref, other_ref, lists_ref,
    color_ref, trans_ref, sig_ref,
    table_ref, feat_ref, a0_ref, a1_ref, w0_ref, w1_ref, coef_ref, rgb_ref, acc_ref,
    place_ref, ids_ref, block_ref,
):
    f32, bf16 = jnp.float32, jnp.bfloat16
    tiles, list_len = lists_ref.shape
    most = list_len // BLOCK
    half = mine_ref.shape[0] // REC_ROWS
    devices = 2 * half
    groups = tiles // 8
    stride = list_len + 8

    found = jnp.int32(0)
    longest = jnp.int32(0)
    for t in range(tiles):
        blocks = (count_ref[t, 0] + BLOCK - 1) // BLOCK
        longest = jnp.maximum(longest, blocks)
        for c in range(most):
            block_ref[found] = t * most + c
            found += (c < blocks).astype(jnp.int32)
    for i in range(UNROLL):
        block_ref[found + i] = tiles * most
    rounds = (found + UNROLL - 1) // UNROLL

    def tile_of(b):
        return lax.div(block_ref[b], most)

    def rows_of(b):
        return pl.ds(pl.multiple_of(block_ref[b] * BLOCK + tile_of(b) * 8, 8), BLOCK)

    def part_of(ref, b):
        return ref[pl.ds(block_ref[b], 1), :]

    me = lax.axis_index(AXES)
    core, far = bits
    ids = lists_ref[...]
    owner = jnp.right_shift(ids, 9)
    place = jnp.zeros_like(ids)
    at = 1
    for bit in range(devices.bit_length() - 1):
        value = bit_of(owner, bit)
        if bit == core:
            where = devices.bit_length() - 2
        elif bit == far:
            where = 0
        else:
            where, at = at, at + 1
        if bit in bits:
            value = jnp.bitwise_xor(value, bit_of(me, bit))
        place += jnp.left_shift(value, where)
    place = jnp.where(ids >= 0, place, -1)
    for value, ref in ((place, place_ref), (ids, ids_ref)):
        for c in range(most):
            ref[pl.ds(c, tiles, stride=most), :] = value[:, c * BLOCK : (c + 1) * BLOCK]
        ref[pl.ds(tiles * most, 8), :] = jnp.full((8, BLOCK), -1, jnp.int32)

    for f in range(FIELDS):
        for q in range(4 if PIECES[f] else 0):
            for part, ref in enumerate((mine_ref, other_ref)):
                rows = ref[pl.ds(4 * f + q, half, stride=REC_ROWS), :]
                for p, piece in enumerate(pieces_of(rows, PIECES[f])):
                    at = (PIECE_AT[f] + p) * 2 * devices + (q // 2) * devices + part * half
                    table_ref[pl.ds(at, half), pl.ds(128 * (q % 2), 128)] = piece

    pixel = lax.broadcasted_iota(jnp.int32, (8, PIXELS), 1)
    which = lax.broadcasted_iota(jnp.int32, (8, PIXELS), 0)
    px = jnp.bitwise_and(pixel, TILE_SIDE - 1).astype(f32) - 7.5
    py = jnp.right_shift(pixel, 4).astype(f32) - 7.5
    feats = jnp.zeros((8, PIXELS), f32)
    for j, value in enumerate((px * px, px * py, py * py, px, py, jnp.ones_like(px))):
        feats = jnp.where(which == j, value, feats)
    feat_ref[...] = jnp.concatenate([feats, feats, feats, jnp.zeros_like(feats)], axis=0).astype(bf16)

    acc_ref[...] = jnp.zeros_like(acc_ref)
    sig_ref[...] = jnp.zeros_like(sig_ref)
    for ref in (w0_ref, w1_ref):
        ref[pl.ds(tiles * stride, BLOCK), :] = jnp.zeros((BLOCK, 128), f32)

    def dark_body(t, _):
        def fill(c, _):
            at = pl.ds(pl.multiple_of(t * stride + c * BLOCK, 8), BLOCK)
            a0_ref[at, :] = jnp.zeros((BLOCK, 128), f32)
            a1_ref[at, :] = jnp.zeros((BLOCK, 128), f32)
            return 0

        return lax.fori_loop((count_ref[t, 0] + BLOCK - 1) // BLOCK, longest, fill, 0)

    lax.fori_loop(0, tiles, dark_body, 0)

    def one_hot(rows, index):
        iota = lax.broadcasted_iota(jnp.int32, (rows, index.shape[1]), 0)
        return (iota == index).astype(f32).astype(bf16)

    wide = 2 * BLOCK
    row8 = lax.broadcasted_iota(jnp.int32, (8, wide), 0)
    second = lax.broadcasted_iota(jnp.int32, (1, wide), 1) >= BLOCK

    def gather(pair):
        ids = jnp.concatenate([part_of(ids_ref, b) for b in pair], axis=1)
        place = jnp.concatenate([part_of(place_ref, b) for b in pair], axis=1)
        row = jnp.where(ids >= 0, bit_of(ids, 8) * devices + place, -1)
        chosen = lax.broadcasted_iota(jnp.int32, (2 * devices, wide), 0) == row
        looked = jnp.dot(table_ref[...], one_hot(256, jnp.bitwise_and(ids, 255)), preferred_element_type=f32)

        def fetch(f):
            total = None
            for p in range(PIECE_AT[f], PIECE_AT[f + 1]):
                piece = looked[p * 2 * devices : (p + 1) * 2 * devices]
                total = piece if total is None else total + piece
            best = jnp.zeros((8, wide), f32)
            for r in range(0, 2 * devices, 8):
                best = jnp.where(chosen[r : r + 8], total[r : r + 8], best)
            return jnp.sum(best, axis=0, keepdims=True)

        fields = []
        sub = lax.broadcasted_iota(jnp.int32, (8, BLOCK), 0)
        for f in range(0, LOOKED, 2):
            halves = []
            for j in range(2):
                here = jnp.broadcast_to(ids[:, BLOCK * j : BLOCK * (j + 1)], (8, BLOCK))
                owner = jnp.broadcast_to(place[:, BLOCK * j : BLOCK * (j + 1)], (8, BLOCK))
                lane = jnp.bitwise_and(here, 127)
                found = jnp.zeros((8, BLOCK), f32)
                for d in range(devices):
                    ref = mine_ref if d < half else other_ref
                    at = (d % half) * REC_ROWS + 4 * f
                    got = jnp.take_along_axis(ref[at : at + 8, :], lane, axis=1, mode="promise_in_bounds")
                    found = jnp.where(owner == d, got, found)
                quarter = jnp.bitwise_and(jnp.right_shift(here, 7), 3)
                halves.append(jnp.where(jnp.bitwise_and(sub, 3) == quarter, found, 0.0))
            both = jnp.concatenate(halves, axis=1)
            fields.append(jnp.sum(both[:4], axis=0, keepdims=True))
            fields.append(jnp.sum(both[4:], axis=0, keepdims=True))
        u, v, ca, cb, cc, log_op, red, green, blue = (fields + [fetch(f) for f in range(LOOKED, FIELDS)])[:FIELDS]
        tids = [tids_ref[jnp.minimum(tile_of(b), tiles - 1)] for b in pair]
        columns = [(off_x + TILE_SIDE // 2 + TILE_SIDE * jnp.bitwise_and(t, WIN_X - 1)).astype(f32) for t in tids]
        lines = [(off_y + TILE_SIDE // 2 + TILE_SIDE * jnp.right_shift(t, 6)).astype(f32) for t in tids]
        du = u - jnp.where(second, columns[1], columns[0])
        dv = v - jnp.where(second, lines[1], lines[0])
        log_op = jnp.where(ids >= 0, log_op, DARK)
        terms = (
            ca,
            cb,
            cc,
            -2.0 * ca * du - cb * dv,
            -2.0 * cc * dv - cb * du,
            ca * du * du + cc * dv * dv + cb * du * dv + log_op,
        )
        coef = jnp.zeros((8, wide), f32)
        for j, value in enumerate(terms):
            coef = jnp.where(row8 == j, value, coef)
        p0, p1, p2 = [p.astype(f32) for p in pieces_of(coef, 3)]
        coefs = jnp.concatenate([p0, p1, p2, jnp.zeros_like(p0)], axis=0).astype(bf16)
        rgb = jnp.zeros((8, wide), f32)
        for j, value in enumerate((red, green, blue)):
            rgb = jnp.where(row8 == j, value, rgb)
        colors = jnp.concatenate([p.astype(f32) for p in pieces_of(rgb, 2)], axis=0).astype(bf16)
        for j, b in enumerate(pair):
            lanes = slice(BLOCK * j, BLOCK * (j + 1))
            coef_ref[pl.ds(pl.multiple_of(b * 32, 32), 32), :] = coefs[:, lanes]
            rgb_ref[pl.ds(pl.multiple_of(b * 16, 16), 16), :] = colors[:, lanes]

    def gather_body(i, _):
        for j in range(0, UNROLL, 2):
            gather((i * UNROLL + j, i * UNROLL + j + 1))
        return 0

    lax.fori_loop(0, rounds, gather_body, 0)

    def alpha_body(i, _):
        for j in range(UNROLL):
            b = i * UNROLL + j
            exponent = lax.dot_general(
                coef_ref[pl.ds(pl.multiple_of(b * 32, 32), 32), :], feat_ref[...],
                (((0,), (0,)), ((), ())), preferred_element_type=f32,
            )
            alpha = jnp.minimum(jnp.exp2(exponent), ALPHA_CAP)
            a0_ref[rows_of(b), :] = alpha[:, :128]
            a1_ref[rows_of(b), :] = alpha[:, 128:]
        return 0

    lax.fori_loop(0, rounds, alpha_body, 0)

    def blend(step, through):
        for j in range(8):
            after = []
            for g in range(groups):
                for h, (a_ref, w_ref) in enumerate(((a0_ref, w0_ref), (a1_ref, w1_ref))):
                    at = pl.ds(g * 8 * stride + step * 8 + j, 8, stride=stride)
                    alpha = a_ref[at, :]
                    before = through[2 * g + h]
                    w_ref[at, :] = before * alpha
                    after.append(before * (1.0 - alpha))
            through = tuple(after)
        return through

    through = (jnp.ones((8, 128), f32),) * (2 * groups)
    through = lax.fori_loop(0, longest * (BLOCK // 8), blend, through)
    for g in range(groups):
        for h in range(2):
            trans_ref[8 * g : 8 * g + 8, 128 * h : 128 * (h + 1)] = through[2 * g + h]

    sig_rows = sig_ref.shape[0]

    def collect_body(i, _):
        left, right = [], []
        for j in range(UNROLL):
            b = i * UNROLL + j
            ids = part_of(ids_ref, b)
            w0, w1 = w0_ref[rows_of(b), :], w1_ref[rows_of(b), :]
            weights = jnp.concatenate(pieces_of(jnp.concatenate([w0, w1], axis=1), 2), axis=0)
            rgb = rgb_ref[pl.ds(pl.multiple_of(b * 16, 16), 16), :]
            at16 = pl.ds(pl.multiple_of(tile_of(b) * 16, 16), 16)
            acc_ref[at16, :] += jnp.dot(
                jnp.concatenate([rgb, rgb], axis=1), weights, preferred_element_type=f32
            )
            sums = jnp.sum((w0 + w1).T, axis=0, keepdims=True)
            hit = lax.broadcasted_iota(jnp.int32, (sig_rows, BLOCK), 0) == jnp.right_shift(ids, 7)
            left.append(
                jnp.concatenate(
                    [jnp.where(hit, p.astype(f32), 0.0).astype(bf16) for p in pieces_of(sums, 2)], axis=0
                )
            )
            right.append(one_hot(128, jnp.bitwise_and(ids, 127)))
        both = lax.dot_general(
            jnp.concatenate(left, axis=1), jnp.concatenate(right, axis=1), (((1,), (1,)), ((), ())),
            preferred_element_type=f32,
        )
        sig_ref[...] += both[:sig_rows] + both[sig_rows:]
        return 0

    lax.fori_loop(0, rounds, collect_body, 0)

    for t in range(tiles):
        color_ref[t] = acc_ref[16 * t : 16 * t + 3, :] + acc_ref[16 * t + 8 : 16 * t + 11, :]
    sig_ref[...] = sig_ref[...] * (1.0 / PIXELS)


def local(bits, gauss_params, tile_ids, tile_lists):
    devices = lax.axis_size(AXES)
    tiles_here, list_len = tile_lists.shape
    core, far = bits
    records, counts = pl.pallas_call(
        project_kernel,
        out_shape=(
            jax.ShapeDtypeStruct((REC_ROWS, 128), jnp.float32),
            jax.ShapeDtypeStruct((tiles_here, 128), jnp.int32),
        ),
    )(gauss_params, tile_lists)
    distant = lax.ppermute(records, AXES, [(d, d ^ (1 << far)) for d in range(devices)])
    room = tiles_here * list_len // BLOCK + max(UNROLL, 8)
    vmem = pl.BlockSpec(memory_space=pltpu.VMEM)
    smem = pl.BlockSpec(memory_space=pltpu.SMEM)
    fixed = (1 << core) | (1 << far)
    members = [
        [d for d in range(devices) if (d & fixed) == kind] for kind in (0, 1 << core, 1 << far, fixed)
    ]
    pair = jnp.stack([records, distant])
    ring = devices // 4
    mine = lax.all_to_all(
        jnp.broadcast_to(pair[None], (ring, 2, REC_ROWS, 128)), AXES, 0, 0, axis_index_groups=members
    ).reshape(2 * ring * REC_ROWS, 128)
    other = lax.ppermute(mine, AXES, [(d, d ^ (1 << core)) for d in range(devices)])

    tiles_total = tiles_here * devices
    win_y = tiles_total // WIN_X
    off_x = (SCREEN_W - WIN_X * TILE_SIDE) // 2
    off_y = (SCREEN_H - win_y * TILE_SIDE) // 2
    sig_rows = devices * gauss_params.shape[1] // 128
    entries = (tiles_here + 1) * (list_len + 8)
    pixel_colors, transmittance, partial_sig = pl.pallas_call(
        functools.partial(render_kernel, off_x, off_y, bits),
        out_shape=(
            jax.ShapeDtypeStruct((tiles_here, 3, PIXELS), jnp.float32),
            jax.ShapeDtypeStruct((tiles_here, PIXELS), jnp.float32),
            jax.ShapeDtypeStruct((sig_rows, 128), jnp.float32),
        ),
        in_specs=[smem, smem, vmem, vmem, vmem],
        out_specs=(vmem, vmem, vmem),
        scratch_shapes=[
            pltpu.VMEM((PIECE_AT[-1] * 2 * devices, 256), jnp.bfloat16),
            pltpu.VMEM((32, PIXELS), jnp.bfloat16),
            pltpu.VMEM((entries, 128), jnp.float32),
            pltpu.VMEM((entries, 128), jnp.float32),
            pltpu.VMEM((entries, 128), jnp.float32),
            pltpu.VMEM((entries, 128), jnp.float32),
            pltpu.VMEM((room * 32, BLOCK), jnp.bfloat16),
            pltpu.VMEM((room * 16, BLOCK), jnp.bfloat16),
            pltpu.VMEM(((tiles_here + 1) * 16, PIXELS), jnp.float32),
            pltpu.VMEM((room, BLOCK), jnp.int32),
            pltpu.VMEM((room, BLOCK), jnp.int32),
            pltpu.SMEM((room,), jnp.int32),
        ],
        compiler_params=pltpu.CompilerParams(vmem_limit_bytes=52 * 2**20),
    )(tile_ids, counts, mine, other, tile_lists)
    swapped = lax.all_to_all(partial_sig.reshape(devices, -1, 128), AXES, 0, 0)
    significance = jnp.sum(swapped, axis=0).reshape(-1)
    return (pixel_colors, transmittance, significance)


def bits_of(mesh):
    flat = list(mesh.devices.flat)
    places = [tuple(getattr(d, "coords", (0,))) for d in flat]

    def reach(bit):
        return sum(abs(p - q) for p, q in zip(places[0], places[1 << bit]))

    bits = range(len(flat).bit_length() - 1)
    core = min(bits, key=reach)
    far = max((b for b in bits if b != core), key=reach)
    return core, far


def solution(mesh):
    return jax.shard_map(
        functools.partial(local, bits_of(mesh)),
        mesh=mesh,
        in_specs=(P(None, AXES), P(AXES), P(AXES, None)),
        out_specs=(P(AXES, None, None), P(AXES, None), P(AXES)),
        check_vma=False,
    )
```

time: 95.9 us -> 54.1 us (0.56)
  Pallas kernels: 59.6 us -> 19.6 us
  blocking collectives: 20.2 us -> 12.3 us
  starting transfers between devices: 4.95 us -> 8.65 us
  waiting for transfers between devices: 8.49 us -> 10.5 us
    pallas_call x1, Pallas kernels: 58.1 us -> 18.1 us  [local(): pl.pallas_call(functools.partial(render_kernel, off_x, off_y, bits), out_...]
    all_to_all x1, blocking collectives: 20.2 us -> 12.3 us  [local(): lax.all_to_all(jnp.broadcast_to(pair[None], (ring, 2, REC_ROWS, 128)), AX...]
    ppermute x1 -> x2, starting transfers between devices: 0.01 us -> 4.04 us  [the longest x1 4.04 us: local(): lax.ppermute(records, AXES, [(d, d ^ 1 << far) for d in range(devices)])]
    ppermute x1 -> x2, waiting for transfers between devices: 1.63 us -> 3.61 us  [the longest x1 1.98 us: local(): lax.ppermute(records, AXES, [(d, d ^ 1 << far) for d in range(devices)])]
  transfers between devices with their start and end apart: 2 -> 3, of which waited for: 2 -> 3; matrix products, arithmetic and copies ran while one was open for 1% -> 1% of each run, Pallas kernels for 0% -> 0%
where the time goes in v3:
time: 54.1 us; the launch traced here: 53.8 us
  Pallas kernels  19.6 us (36%)
  blocking collectives  12.3 us (23%)
  waiting for transfers between devices  10.5 us (19%)
  starting transfers between devices  8.65 us (16%)
  other arithmetic  1.35 us (2%)
  local copies, waits for them, and re-layouts  0.67 us (1%)
  between operations  0.67 us (1%)
    pallas_call x1, Pallas kernels, local(): pl.pallas_call(functools.partial(render_kernel, off_x, off_y, bits), out_...  18.1 us
    all_to_all x1, blocking collectives, local(): lax.all_to_all(jnp.broadcast_to(pair[None], (ring, 2, REC_ROWS, 128)), AX...  12.3 us
    all_to_all x1, waiting for transfers between devices, local(): swapped = lax.all_to_all(partial_sig.reshape(devices, -1, 128), AXES, 0, 0)  6.87 us
    all_to_all x1, starting transfers between devices, local(): swapped = lax.all_to_all(partial_sig.reshape(devices, -1, 128), AXES, 0, 0)  4.61 us
    ppermute x1, starting transfers between devices, local(): lax.ppermute(records, AXES, [(d, d ^ 1 << far) for d in range(devices)])  4.04 us
    ppermute x1, waiting for transfers between devices, local(): lax.ppermute(records, AXES, [(d, d ^ 1 << far) for d in range(devices)])  1.98 us
    ppermute x1, waiting for transfers between devices, local(): lax.ppermute(mine, AXES, [(d, d ^ 1 << core) for d in range(devices)])  1.63 us
    pallas_call x1, Pallas kernels, local(): pl.pallas_call(project_kernel, out_shape=(jax.ShapeDtypeStruct((REC_ROWS,...  1.55 us
  transfers between devices with their start and end apart: 3, of which 3 were waited for; matrix products, arithmetic and copies ran while one was open for 1% of the time, Pallas kernels for 0%

profile of v3, /device:TPU:0, one launch (start us, length us, event | category | flops | bytes accessed | tf_op | source)
XLA Modules:
  0.0 53.8 jit_solution(5186554277328305620)
XLA Ops:
  0.6 1.5 %shard_map.58 = (f32[40,128]{1,0:T(8,128)}, s32[16,128]{1,0:T(8,128)}) custom-call(f32[14,512]{1,0:T(8,128)} %params_ref.1, s32[16,1024]{1,0:T(8,128)} %lists_ref.3), custom_call_target="tpu_custom_call" | custom-call | tf_op jit(solution)/shard_map/pallas_call | solution.py:331
  2.2 4.0 %collective-permute-start = (f32[40,128]{1,0:T(8,128)}, f32[40,128]{1,0:T(8,128)S(1)}, u32[]{:S(2)}, u32[]{:S(2)}) collective-permute-start(f32[40,128]{1,0:T(8,128)} %get-tuple-element.9), channel_id=1, source_target_pairs={{0,2},{1,3},{2,0},{3,1},{4,6},{5,7},{6,4},{7,5},{8,10},{9,11},{10,... | collective-permute-start | bytes 61448 | tf_op jit(solution)/shard_map/ppermute | solution.py:338
  6.2 2.0 %collective-permute-done = f32[40,128]{1,0:T(8,128)S(1)} collective-permute-done((f32[40,128]{1,0:T(8,128)}, f32[40,128]{1,0:T(8,128)S(1)}, u32[]{:S(2)}, u32[]{:S(2)}) %collective-permute-start) | collective-permute-done | bytes 20512 | tf_op jit(solution)/shard_map/ppermute | solution.py:338
  8.2 0.7 %pad_maximum_fusion = f32[2,40,128]{2,1,0:T(8,128)S(1)} fusion(f32[1,40,128]{2,1,0:T(8,128)S(1)} %bitcast.8, f32[1,40,128]{2,1,0:T(8,128)} %bitcast.7), kind=kLoop, calls=%fused_computation | loop fusion | flops 10240 | bytes 81920 | tf_op jit(solution)/shard_map/stack | solution.py:346
  9.0 0.0 copy-start
  9.0 0.0 copy-start.1
  9.0 12.3 %all_to_all.10 = f32[8,2,40,128]{3,2,1,0:T(8,128)S(1)} all-to-all(f32[8,2,40,128]{3,2,1,0:T(8,128)S(1)} %broadcast_in_dim.2), channel_id=1, replica_groups={{0,1,8,9,16,17,24,25},{4,5,12,13,20,21,28,29},{2,3,10,11,18,19,26,27},{..., dimensions={0} | all-to-all | bytes 655360 | tf_op jit(solution)/shard_map/all_to_all | solution.py:348
  21.3 0.0 copy-start.2
  21.3 0.0 collective-permute-start.1
  21.3 1.6 %collective-permute-done.1.other_ref = f32[640,128]{1,0:T(8,128)S(1)} collective-permute-done((f32[640,128]{1,0:T(8,128)S(1)}, f32[640,128]{1,0:T(8,128)S(1)}, u32[]{:S(2)}, u32[]{:S(2)}) %collective-permute-start.1) | collective-permute-done | bytes 327712 | tf_op jit(solution)/shard_map/ppermute | solution.py:351
  22.9 0.0 copy-done
  22.9 0.0 copy-done.1
  22.9 0.0 copy-done.2
  22.9 18.1 %shard_map.59 = (f32[16,3,256]{2,1,0:T(4,128)S(1)}, f32[16,256]{1,0:T(8,128)}, f32[128,128]{1,0:T(8,128)}) custom-call(s32[16]{0:T(128)S(1)} %copy-done.2, s32[16,128]{1,0:T(8,128)S(1)} %copy-done.1, f32[640,128]{1,0:T(8,128)S(1)} %bitcast.6, f32[640,128]{1,0:T(8,128)S(1)} %collective-permute-done.1.other_ref, s32[16,1024]{1,0:T(8,128)S(1)} %copy-done), custom_call_target="tpu_custom_call" | custom-call | tf_op jit(solution)/shard_map/pallas_call | solution.py:359
  41.0 4.6 %all-to-all-start.1 = ((f32[32,4,128]{2,1,0:T(4,128)}), f32[32,4,128]{2,1,0:T(4,128)S(1)}, u32[]{:S(2)}, u32[]{:S(2)}) async-start(f32[32,4,128]{2,1,0:T(4,128)} %bitcast.3), calls=%async_computation.1 | async-start | bytes 131072 | tf_op jit(solution)/shard_map/all_to_all | solution.py:384
  45.6 0.6 %copy.6 = f32[16,3,256]{2,0,1:T(8,128)} copy(f32[16,3,256]{2,1,0:T(4,128)S(1)} %get-tuple-element.13) | data formatting | bytes 98304
  46.3 6.9 %all-to-all-done.1 = f32[32,4,128]{2,1,0:T(4,128)S(1)} async-done(((f32[32,4,128]{2,1,0:T(4,128)}), f32[32,4,128]{2,1,0:T(4,128)S(1)}, u32[]{:S(2)}, u32[]{:S(2)}) %all-to-all-start.1) | async-done | bytes 65568 | tf_op jit(solution)/shard_map/all_to_all | solution.py:384
  53.1 0.6 %reduce_sum.9 = f32[4,128]{1,0:T(4,128)} reduce(f32[32,4,128]{2,1,0:T(4,128)S(1)} %all-to-all-done.1, f32[]{:T(128)} %constant.0.clone.1), dimensions={0}, to_apply=%region_0.0 | reduce | flops 15872 | bytes 67588 | tf_op jit(solution)/shard_map/reduce_sum | solution.py:385
  (1 shorter events, 0.0 us)
Async XLA Ops:
  2.2 6.0 %collective-permute-start = (f32[40,128]{1,0:T(8,128)}, f32[40,128]{1,0:T(8,128)S(1)}, u32[]{:S(2)}, u32[]{:S(2)}) collective-permute-start(f32[40,128]{1,0:T(8,128)} %get-tuple-element.9), channel_id=1, source_target_pairs={{0,2},{1,3},{2,0},{3,1},{4,6},{5,7},{6,4},{7,5},{8,10},{9,11},{10,... | collective-permute-start | bytes 61448 | tf_op jit(solution)/shard_map/ppermute | solution.py:338
  9.0 14.0 %copy-start = (s32[16,1024]{1,0:T(8,128)S(1)}, s32[16,1024]{1,0:T(8,128)}, u32[]{:S(2)}) copy-start(s32[16,1024]{1,0:T(8,128)} %lists_ref.3) | copy-start | bytes 196612
  9.0 14.0 %copy-start.1 = (s32[16,128]{1,0:T(8,128)S(1)}, s32[16,128]{1,0:T(8,128)}, u32[]{:S(2)}) copy-start(s32[16,128]{1,0:T(8,128)} %get-tuple-element.8.count_ref) | copy-start | bytes 24580
  21.3 1.6 %copy-start.2 = (s32[16]{0:T(128)S(1)}, s32[16]{0:T(128)}, u32[]{:S(2)}) copy-start(s32[16]{0:T(128)} %tids_ref.1) | copy-start | bytes 196
  21.3 1.6 %collective-permute-start.1 = (f32[640,128]{1,0:T(8,128)S(1)}, f32[640,128]{1,0:T(8,128)S(1)}, u32[]{:S(2)}, u32[]{:S(2)}) collective-permute-start(f32[640,128]{1,0:T(8,128)S(1)} %bitcast.5), channel_id=1, source_target_pairs={{0,4},{1,5},{2,6},{3,7},{4,0},{5,1},{6,2},{7,3},{8,12},{9,13},{10,... | collective-permute-start | bytes 983048 | tf_op jit(solution)/shard_map/ppermute | solution.py:351
  41.0 12.1 %all-to-all-start.1 = ((f32[32,4,128]{2,1,0:T(4,128)}), f32[32,4,128]{2,1,0:T(4,128)S(1)}, u32[]{:S(2)}, u32[]{:S(2)}) async-start(f32[32,4,128]{2,1,0:T(4,128)} %bitcast.3), calls=%async_computation.1 | async-start | bytes 131072 | tf_op jit(solution)/shard_map/all_to_all | solution.py:384

commit v4 on v3

--- a/solution.py
+++ b/solution.py
@@ -14,6 +14,9 @@
 PIXELS = TILE_SIDE * TILE_SIDE
 BLOCK = 128
 UNROLL = 8
+GATHER_STEP = 32
+ALPHA_STEP = 32
+COLLECT_STEP = 32
 FIELDS = 9
 REC_ROWS = 40
 LOOKED = 2
@@ -108,7 +111,12 @@
             found += (c < blocks).astype(jnp.int32)
     for i in range(UNROLL):
         block_ref[found + i] = tiles * most
-    rounds = (found + UNROLL - 1) // UNROLL
+
+    def in_steps(body, size):
+        whole = lax.div(found, size)
+        lax.fori_loop(0, whole, lambda i, _: body(i * size, size), 0)
+        rest = lax.div(found + UNROLL - 1, UNROLL)
+        lax.fori_loop(whole * (size // UNROLL), rest, lambda i, _: body(i * UNROLL, UNROLL), 0)
 
     def tile_of(b):
         return lax.div(block_ref[b], most)
@@ -248,16 +256,16 @@
             coef_ref[pl.ds(pl.multiple_of(b * 32, 32), 32), :] = coefs[:, lanes]
             rgb_ref[pl.ds(pl.multiple_of(b * 16, 16), 16), :] = colors[:, lanes]
 
-    def gather_body(i, _):
-        for j in range(0, UNROLL, 2):
-            gather((i * UNROLL + j, i * UNROLL + j + 1))
+    def gather_body(first, size):
+        for j in range(0, size, 2):
+            gather((first + j, first + j + 1))
         return 0
 
-    lax.fori_loop(0, rounds, gather_body, 0)
-
-    def alpha_body(i, _):
-        for j in range(UNROLL):
-            b = i * UNROLL + j
+    in_steps(gather_body, GATHER_STEP)
+
+    def alpha_body(first, size):
+        for j in range(size):
+            b = first + j
             exponent = lax.dot_general(
                 coef_ref[pl.ds(pl.multiple_of(b * 32, 32), 32), :], feat_ref[...],
                 (((0,), (0,)), ((), ())), preferred_element_type=f32,
@@ -267,7 +275,7 @@
             a1_ref[rows_of(b), :] = alpha[:, 128:]
         return 0
 
-    lax.fori_loop(0, rounds, alpha_body, 0)
+    in_steps(alpha_body, ALPHA_STEP)
 
     def blend(step, through):
         for j in range(8):
@@ -290,10 +298,10 @@
 
     sig_rows = sig_ref.shape[0]
 
-    def collect_body(i, _):
+    def collect_body(first, size):
         left, right = [], []
-        for j in range(UNROLL):
-            b = i * UNROLL + j
+        for j in range(size):
+            b = first + j
             ids = part_of(ids_ref, b)
             w0, w1 = w0_ref[rows_of(b), :], w1_ref[rows_of(b), :]
             weights = jnp.concatenate(pieces_of(jnp.concatenate([w0, w1], axis=1), 2), axis=0)
@@ -317,7 +325,7 @@
         sig_ref[...] += both[:sig_rows] + both[sig_rows:]
         return 0
 
-    lax.fori_loop(0, rounds, collect_body, 0)
+    in_steps(collect_body, COLLECT_STEP)
 
     for t in range(tiles):
         color_ref[t] = acc_ref[16 * t : 16 * t + 3, :] + acc_ref[16 * t + 8 : 16 * t + 11, :]
@@ -331,9 +339,10 @@
     records, counts = pl.pallas_call(
         project_kernel,
         out_shape=(
-            jax.ShapeDtypeStruct((REC_ROWS, 128), jnp.float32),
+            pltpu.VMEM((REC_ROWS, 128), jnp.float32),
             jax.ShapeDtypeStruct((tiles_here, 128), jnp.int32),
         ),
+        out_specs=(pl.BlockSpec(memory_space=pltpu.VMEM),) * 2,
     )(gauss_params, tile_lists)
     distant = lax.ppermute(records, AXES, [(d, d ^ (1 << far)) for d in range(devices)])
     room = tiles_here * list_len // BLOCK + max(UNROLL, 8)

time: 54.1 us -> 50.3 us (0.930)
  Pallas kernels: 19.6 us -> 16.8 us
  other arithmetic: 1.35 us -> 0.62 us
    pallas_call x1, Pallas kernels: 18.1 us -> 15.3 us  [local(): pl.pallas_call(functools.partial(render_kernel, off_x, off_y, bits), out_...]
    another operation x1, other arithmetic: 0.73 us -> 0.01 us  [local(): pair = jnp.stack([records, distant])]
where the time goes in v4:
time: 50.3 us; the launch traced here: 50 us
  Pallas kernels  16.8 us (33%)
  blocking collectives  12.3 us (24%)
  waiting for transfers between devices  10.3 us (20%)
  starting transfers between devices  8.64 us (17%)
  local copies, waits for them, and re-layouts  0.67 us (1%)
  between operations  0.67 us (1%)
  other arithmetic  0.62 us (1%)
    pallas_call x1, Pallas kernels, local(): pl.pallas_call(functools.partial(render_kernel, off_x, off_y, bits), out_...  15.3 us
    all_to_all x1, blocking collectives, local(): lax.all_to_all(jnp.broadcast_to(pair[None], (ring, 2, REC_ROWS, 128)), AX...  12.3 us
    all_to_all x1, waiting for transfers between devices, local(): swapped = lax.all_to_all(partial_sig.reshape(devices, -1, 128), AXES, 0, 0)  6.87 us
    all_to_all x1, starting transfers between devices, local(): swapped = lax.all_to_all(partial_sig.reshape(devices, -1, 128), AXES, 0, 0)  4.6 us
    ppermute x1, starting transfers between devices, local(): lax.ppermute(records, AXES, [(d, d ^ 1 << far) for d in range(devices)])  4.04 us
    ppermute x1, waiting for transfers between devices, local(): lax.ppermute(records, AXES, [(d, d ^ 1 << far) for d in range(devices)])  1.77 us
    ppermute x1, waiting for transfers between devices, local(): lax.ppermute(mine, AXES, [(d, d ^ 1 << core) for d in range(devices)])  1.63 us
    pallas_call x1, Pallas kernels, local(): pl.pallas_call(project_kernel, out_shape=(pltpu.VMEM((REC_ROWS, 128), jnp...  1.57 us
  transfers between devices with their start and end apart: 3, of which 3 were waited for; matrix products, arithmetic and copies ran while one was open for 1% of the time, Pallas kernels for 0%

profile of v4, /device:TPU:0, one launch (start us, length us, event | category | flops | bytes accessed | tf_op | source)
XLA Modules:
  0.0 50.0 jit_solution(4779044781436004550)
XLA Ops:
  0.6 1.6 %shard_map.58 = (f32[40,128]{1,0:T(8,128)S(1)}, s32[16,128]{1,0:T(8,128)}) custom-call(f32[14,512]{1,0:T(8,128)} %params_ref.1, s32[16,1024]{1,0:T(8,128)} %lists_ref.3), custom_call_target="tpu_custom_call" | custom-call | tf_op jit(solution)/shard_map/pallas_call | solution.py:339
  2.2 4.0 %collective-permute-start = (f32[40,128]{1,0:T(8,128)S(1)}, f32[40,128]{1,0:T(8,128)S(1)}, u32[]{:S(2)}, u32[]{:S(2)}) collective-permute-start(f32[40,128]{1,0:T(8,128)S(1)} %get-tuple-element.9), channel_id=1, source_target_pairs={{0,2},{1,3},{2,0},{3,1},{4,6},{5,7},{6,4},{7,5},{8,10},{9,11},{10,... | collective-permute-start | bytes 61448 | tf_op jit(solution)/shard_map/ppermute | solution.py:347
  6.2 1.8 %collective-permute-done = f32[40,128]{1,0:T(8,128)S(1)} collective-permute-done((f32[40,128]{1,0:T(8,128)S(1)}, f32[40,128]{1,0:T(8,128)S(1)}, u32[]{:S(2)}, u32[]{:S(2)}) %collective-permute-start) | collective-permute-done | bytes 20512 | tf_op jit(solution)/shard_map/ppermute | solution.py:347
  8.0 0.0 copy-start
  8.0 0.0 copy-start.1
  8.1 12.3 %all_to_all.10 = f32[8,2,40,128]{3,2,1,0:T(8,128)S(1)} all-to-all(f32[8,2,40,128]{3,2,1,0:T(8,128)S(1)} %broadcast_in_dim.2), channel_id=1, replica_groups={{0,1,8,9,16,17,24,25},{4,5,12,13,20,21,28,29},{2,3,10,11,18,19,26,27},{..., dimensions={0} | all-to-all | bytes 655360 | tf_op jit(solution)/shard_map/all_to_all | solution.py:357
  20.4 0.0 copy-start.2
  20.4 0.0 collective-permute-start.1
  20.4 1.6 %collective-permute-done.1.other_ref = f32[640,128]{1,0:T(8,128)S(1)} collective-permute-done((f32[640,128]{1,0:T(8,128)S(1)}, f32[640,128]{1,0:T(8,128)S(1)}, u32[]{:S(2)}, u32[]{:S(2)}) %collective-permute-start.1) | collective-permute-done | bytes 327712 | tf_op jit(solution)/shard_map/ppermute | solution.py:360
  22.0 0.0 copy-done
  22.0 0.0 copy-done.1
  22.0 0.0 copy-done.2
  22.0 15.3 %shard_map.59 = (f32[16,3,256]{2,1,0:T(4,128)S(1)}, f32[16,256]{1,0:T(8,128)}, f32[128,128]{1,0:T(8,128)}) custom-call(s32[16]{0:T(128)S(1)} %copy-done.2, s32[16,128]{1,0:T(8,128)S(1)} %copy-done.1, f32[640,128]{1,0:T(8,128)S(1)} %bitcast.6, f32[640,128]{1,0:T(8,128)S(1)} %collective-permute-done.1.other_ref, s32[16,1024]{1,0:T(8,128)S(1)} %copy-done), custom_call_target="tpu_custom_call" | custom-call | tf_op jit(solution)/shard_map/pallas_call | solution.py:368
  37.3 4.6 %all-to-all-start.1 = ((f32[32,4,128]{2,1,0:T(4,128)}), f32[32,4,128]{2,1,0:T(4,128)S(1)}, u32[]{:S(2)}, u32[]{:S(2)}) async-start(f32[32,4,128]{2,1,0:T(4,128)} %bitcast.3), calls=%async_computation.1 | async-start | bytes 131072 | tf_op jit(solution)/shard_map/all_to_all | solution.py:393
  41.9 0.6 %copy.6 = f32[16,3,256]{2,0,1:T(8,128)} copy(f32[16,3,256]{2,1,0:T(4,128)S(1)} %get-tuple-element.13) | data formatting | bytes 98304
  42.5 6.9 %all-to-all-done.1 = f32[32,4,128]{2,1,0:T(4,128)S(1)} async-done(((f32[32,4,128]{2,1,0:T(4,128)}), f32[32,4,128]{2,1,0:T(4,128)S(1)}, u32[]{:S(2)}, u32[]{:S(2)}) %all-to-all-start.1) | async-done | bytes 65568 | tf_op jit(solution)/shard_map/all_to_all | solution.py:393
  49.4 0.6 %reduce_sum.9 = f32[4,128]{1,0:T(4,128)} reduce(f32[32,4,128]{2,1,0:T(4,128)S(1)} %all-to-all-done.1, f32[]{:T(128)} %constant.0.clone.1), dimensions={0}, to_apply=%region_0.0 | reduce | flops 15872 | bytes 67588 | tf_op jit(solution)/shard_map/reduce_sum | solution.py:394
  (2 shorter events, 0.0 us)
Async XLA Ops:
  2.2 5.8 %collective-permute-start = (f32[40,128]{1,0:T(8,128)S(1)}, f32[40,128]{1,0:T(8,128)S(1)}, u32[]{:S(2)}, u32[]{:S(2)}) collective-permute-start(f32[40,128]{1,0:T(8,128)S(1)} %get-tuple-element.9), channel_id=1, source_target_pairs={{0,2},{1,3},{2,0},{3,1},{4,6},{5,7},{6,4},{7,5},{8,10},{9,11},{10,... | collective-permute-start | bytes 61448 | tf_op jit(solution)/shard_map/ppermute | solution.py:347
  8.0 14.0 %copy-start = (s32[16,1024]{1,0:T(8,128)S(1)}, s32[16,1024]{1,0:T(8,128)}, u32[]{:S(2)}) copy-start(s32[16,1024]{1,0:T(8,128)} %lists_ref.3) | copy-start | bytes 196612
  8.0 14.0 %copy-start.1 = (s32[16,128]{1,0:T(8,128)S(1)}, s32[16,128]{1,0:T(8,128)}, u32[]{:S(2)}) copy-start(s32[16,128]{1,0:T(8,128)} %get-tuple-element.8.count_ref) | copy-start | bytes 24580
  20.4 1.6 %copy-start.2 = (s32[16]{0:T(128)S(1)}, s32[16]{0:T(128)}, u32[]{:S(2)}) copy-start(s32[16]{0:T(128)} %tids_ref.1) | copy-start | bytes 196
  20.4 1.6 %collective-permute-start.1 = (f32[640,128]{1,0:T(8,128)S(1)}, f32[640,128]{1,0:T(8,128)S(1)}, u32[]{:S(2)}, u32[]{:S(2)}) collective-permute-start(f32[640,128]{1,0:T(8,128)S(1)} %bitcast.5), channel_id=1, source_target_pairs={{0,4},{1,5},{2,6},{3,7},{4,0},{5,1},{6,2},{7,3},{8,12},{9,13},{10,... | collective-permute-start | bytes 983048 | tf_op jit(solution)/shard_map/ppermute | solution.py:360
  37.3 12.1 %all-to-all-start.1 = ((f32[32,4,128]{2,1,0:T(4,128)}), f32[32,4,128]{2,1,0:T(4,128)S(1)}, u32[]{:S(2)}, u32[]{:S(2)}) async-start(f32[32,4,128]{2,1,0:T(4,128)} %bitcast.3), calls=%async_computation.1 | async-start | bytes 131072 | tf_op jit(solution)/shard_map/all_to_all | solution.py:393

commit v5 on v4

--- a/solution.py
+++ b/solution.py
@@ -14,9 +14,9 @@
 PIXELS = TILE_SIDE * TILE_SIDE
 BLOCK = 128
 UNROLL = 8
-GATHER_STEP = 32
-ALPHA_STEP = 32
-COLLECT_STEP = 32
+GATHER_STEP = 64
+ALPHA_STEP = 64
+COLLECT_STEP = 64
 FIELDS = 9
 REC_ROWS = 40
 LOOKED = 2
@@ -113,10 +113,15 @@
         block_ref[found + i] = tiles * most
 
     def in_steps(body, size):
-        whole = lax.div(found, size)
-        lax.fori_loop(0, whole, lambda i, _: body(i * size, size), 0)
-        rest = lax.div(found + UNROLL - 1, UNROLL)
-        lax.fori_loop(whole * (size // UNROLL), rest, lambda i, _: body(i * UNROLL, UNROLL), 0)
+        units = lax.div(found + UNROLL - 1, UNROLL)
+        done = 0
+        while size >= UNROLL:
+            share = size // UNROLL
+            first = done // share if isinstance(done, int) else lax.div(done, share)
+            last = lax.div(units, share)
+            lax.fori_loop(first, last, lambda i, _, size=size: body(i * size, size), 0)
+            done = last * share
+            size //= 2
 
     def tile_of(b):
         return lax.div(block_ref[b], most)
@@ -184,8 +189,9 @@
     lax.fori_loop(0, tiles, dark_body, 0)
 
     def one_hot(rows, index):
-        iota = lax.broadcasted_iota(jnp.int32, (rows, index.shape[1]), 0)
-        return (iota == index).astype(f32).astype(bf16)
+        here = jnp.where((index >= 0) & (index < rows), index, -1).astype(f32).astype(bf16)
+        iota = lax.broadcasted_iota(jnp.int32, (rows, index.shape[1]), 0).astype(f32).astype(bf16)
+        return jnp.where(iota == here, jnp.array(1, bf16), jnp.array(0, bf16))
 
     wide = 2 * BLOCK
     row8 = lax.broadcasted_iota(jnp.int32, (8, wide), 0)

time: 50.3 us -> 49.1 us (0.976); the launches traced: 50 us -> 48.2 us
  starting transfers between devices: 8.64 us -> 7.33 us
    all_to_all x1, starting transfers between devices: 4.6 us -> 3.29 us  [local(): swapped = lax.all_to_all(partial_sig.reshape(devices, -1, 128), AXES, 0, 0)]
    pallas_call x1, Pallas kernels: 15.3 us -> 14.7 us  [local(): pl.pallas_call(functools.partial(render_kernel, off_x, off_y, bits), out_...]
where the time goes in v5:
time: 49.1 us; the launch traced here: 48.2 us
  Pallas kernels  16.3 us (33%)
  blocking collectives  12.3 us (25%)
  waiting for transfers between devices  10.3 us (21%)
  starting transfers between devices  7.33 us (15%)
  local copies, waits for them, and re-layouts  0.67 us (1%)
  between operations  0.67 us (1%)
  other arithmetic  0.62 us (1%)
    pallas_call x1, Pallas kernels, local(): pl.pallas_call(functools.partial(render_kernel, off_x, off_y, bits), out_...  14.7 us
    all_to_all x1, blocking collectives, local(): lax.all_to_all(jnp.broadcast_to(pair[None], (ring, 2, REC_ROWS, 128)), AX...  12.3 us
    all_to_all x1, waiting for transfers between devices, local(): swapped = lax.all_to_all(partial_sig.reshape(devices, -1, 128), AXES, 0, 0)  6.87 us
    ppermute x1, starting transfers between devices, local(): lax.ppermute(records, AXES, [(d, d ^ 1 << far) for d in range(devices)])  4.04 us
    all_to_all x1, starting transfers between devices, local(): swapped = lax.all_to_all(partial_sig.reshape(devices, -1, 128), AXES, 0, 0)  3.29 us
    ppermute x1, waiting for transfers between devices, local(): lax.ppermute(records, AXES, [(d, d ^ 1 << far) for d in range(devices)])  1.77 us
    ppermute x1, waiting for transfers between devices, local(): lax.ppermute(mine, AXES, [(d, d ^ 1 << core) for d in range(devices)])  1.63 us
    pallas_call x1, Pallas kernels, local(): pl.pallas_call(project_kernel, out_shape=(pltpu.VMEM((REC_ROWS, 128), jnp...  1.57 us
  transfers between devices with their start and end apart: 3, of which 3 were waited for; matrix products, arithmetic and copies ran while one was open for 1% of the time, Pallas kernels for 0%

profile of v5, /device:TPU:0, one launch (start us, length us, event | category | flops | bytes accessed | tf_op | source)
XLA Modules:
  0.0 48.2 jit_solution(16514601697457053101)
XLA Ops:
  0.6 1.6 %shard_map.58 = (f32[40,128]{1,0:T(8,128)S(1)}, s32[16,128]{1,0:T(8,128)}) custom-call(f32[14,512]{1,0:T(8,128)} %params_ref.1, s32[16,1024]{1,0:T(8,128)} %lists_ref.3), custom_call_target="tpu_custom_call" | custom-call | tf_op jit(solution)/shard_map/pallas_call | solution.py:345
  2.2 4.0 %collective-permute-start = (f32[40,128]{1,0:T(8,128)S(1)}, f32[40,128]{1,0:T(8,128)S(1)}, u32[]{:S(2)}, u32[]{:S(2)}) collective-permute-start(f32[40,128]{1,0:T(8,128)S(1)} %get-tuple-element.9), channel_id=1, source_target_pairs={{0,2},{1,3},{2,0},{3,1},{4,6},{5,7},{6,4},{7,5},{8,10},{9,11},{10,... | collective-permute-start | bytes 61448 | tf_op jit(solution)/shard_map/ppermute | solution.py:353
  6.2 1.8 %collective-permute-done = f32[40,128]{1,0:T(8,128)S(1)} collective-permute-done((f32[40,128]{1,0:T(8,128)S(1)}, f32[40,128]{1,0:T(8,128)S(1)}, u32[]{:S(2)}, u32[]{:S(2)}) %collective-permute-start) | collective-permute-done | bytes 20512 | tf_op jit(solution)/shard_map/ppermute | solution.py:353
  8.0 0.0 copy-start
  8.0 0.0 copy-start.1
  8.1 12.3 %all_to_all.10 = f32[8,2,40,128]{3,2,1,0:T(8,128)S(1)} all-to-all(f32[8,2,40,128]{3,2,1,0:T(8,128)S(1)} %broadcast_in_dim.2), channel_id=1, replica_groups={{0,1,8,9,16,17,24,25},{4,5,12,13,20,21,28,29},{2,3,10,11,18,19,26,27},{..., dimensions={0} | all-to-all | bytes 655360 | tf_op jit(solution)/shard_map/all_to_all | solution.py:363
  20.4 0.0 copy-start.2
  20.4 0.0 collective-permute-start.1
  20.4 1.6 %collective-permute-done.1.other_ref = f32[640,128]{1,0:T(8,128)S(1)} collective-permute-done((f32[640,128]{1,0:T(8,128)S(1)}, f32[640,128]{1,0:T(8,128)S(1)}, u32[]{:S(2)}, u32[]{:S(2)}) %collective-permute-start.1) | collective-permute-done | bytes 327712 | tf_op jit(solution)/shard_map/ppermute | solution.py:366
  22.0 0.0 copy-done
  22.0 0.0 copy-done.1
  22.0 0.0 copy-done.2
  22.0 14.7 %shard_map.59 = (f32[16,3,256]{2,1,0:T(4,128)S(1)}, f32[16,256]{1,0:T(8,128)}, f32[128,128]{1,0:T(8,128)}) custom-call(s32[16]{0:T(128)S(1)} %copy-done.2, s32[16,128]{1,0:T(8,128)S(1)} %copy-done.1, f32[640,128]{1,0:T(8,128)S(1)} %bitcast.6, f32[640,128]{1,0:T(8,128)S(1)} %collective-permute-done.1.other_ref, s32[16,1024]{1,0:T(8,128)S(1)} %copy-done), custom_call_target="tpu_custom_call" | custom-call | tf_op jit(solution)/shard_map/pallas_call | solution.py:374
  36.8 3.3 %all-to-all-start.1 = ((f32[32,4,128]{2,1,0:T(4,128)}), f32[32,4,128]{2,1,0:T(4,128)S(1)}, u32[]{:S(2)}, u32[]{:S(2)}) async-start(f32[32,4,128]{2,1,0:T(4,128)} %bitcast.3), calls=%async_computation.1 | async-start | bytes 131072 | tf_op jit(solution)/shard_map/all_to_all | solution.py:399
  40.1 0.6 %copy.6 = f32[16,3,256]{2,0,1:T(8,128)} copy(f32[16,3,256]{2,1,0:T(4,128)S(1)} %get-tuple-element.13) | data formatting | bytes 98304
  40.7 6.9 %all-to-all-done.1 = f32[32,4,128]{2,1,0:T(4,128)S(1)} async-done(((f32[32,4,128]{2,1,0:T(4,128)}), f32[32,4,128]{2,1,0:T(4,128)S(1)}, u32[]{:S(2)}, u32[]{:S(2)}) %all-to-all-start.1) | async-done | bytes 65568 | tf_op jit(solution)/shard_map/all_to_all | solution.py:399
  47.5 0.6 %reduce_sum.9 = f32[4,128]{1,0:T(4,128)} reduce(f32[32,4,128]{2,1,0:T(4,128)S(1)} %all-to-all-done.1, f32[]{:T(128)} %constant.0.clone.1), dimensions={0}, to_apply=%region_0.0 | reduce | flops 15872 | bytes 67588 | tf_op jit(solution)/shard_map/reduce_sum | solution.py:400
  (2 shorter events, 0.0 us)
Async XLA Ops:
  2.2 5.8 %collective-permute-start = (f32[40,128]{1,0:T(8,128)S(1)}, f32[40,128]{1,0:T(8,128)S(1)}, u32[]{:S(2)}, u32[]{:S(2)}) collective-permute-start(f32[40,128]{1,0:T(8,128)S(1)} %get-tuple-element.9), channel_id=1, source_target_pairs={{0,2},{1,3},{2,0},{3,1},{4,6},{5,7},{6,4},{7,5},{8,10},{9,11},{10,... | collective-permute-start | bytes 61448 | tf_op jit(solution)/shard_map/ppermute | solution.py:353
  8.0 14.0 %copy-start = (s32[16,1024]{1,0:T(8,128)S(1)}, s32[16,1024]{1,0:T(8,128)}, u32[]{:S(2)}) copy-start(s32[16,1024]{1,0:T(8,128)} %lists_ref.3) | copy-start | bytes 196612
  8.0 14.0 %copy-start.1 = (s32[16,128]{1,0:T(8,128)S(1)}, s32[16,128]{1,0:T(8,128)}, u32[]{:S(2)}) copy-start(s32[16,128]{1,0:T(8,128)} %get-tuple-element.8.count_ref) | copy-start | bytes 24580
  20.4 1.6 %copy-start.2 = (s32[16]{0:T(128)S(1)}, s32[16]{0:T(128)}, u32[]{:S(2)}) copy-start(s32[16]{0:T(128)} %tids_ref.1) | copy-start | bytes 196
  20.4 1.6 %collective-permute-start.1 = (f32[640,128]{1,0:T(8,128)S(1)}, f32[640,128]{1,0:T(8,128)S(1)}, u32[]{:S(2)}, u32[]{:S(2)}) collective-permute-start(f32[640,128]{1,0:T(8,128)S(1)} %bitcast.5), channel_id=1, source_target_pairs={{0,4},{1,5},{2,6},{3,7},{4,0},{5,1},{6,2},{7,3},{8,12},{9,13},{10,... | collective-permute-start | bytes 983048 | tf_op jit(solution)/shard_map/ppermute | solution.py:366
  36.8 10.8 %all-to-all-start.1 = ((f32[32,4,128]{2,1,0:T(4,128)}), f32[32,4,128]{2,1,0:T(4,128)S(1)}, u32[]{:S(2)}, u32[]{:S(2)}) async-start(f32[32,4,128]{2,1,0:T(4,128)} %bitcast.3), calls=%async_computation.1 | async-start | bytes 131072 | tf_op jit(solution)/shard_map/all_to_all | solution.py:399
